TPU v7x, 512 devices: a whole 4x4x16 slice. The times are simulated.
512 devices in a mesh: row: 16 (over x_hi, y, core), col: 32 (over x_lo, z).
Axes of the slice: x: 4 (x_hi: 2, x_lo: 2; x = x_hi * 2 + x_lo), y: 4, z: 16, core: 2. Of those that a mesh axis runs over, the one named last changes fastest.
Arguments:
- gradient: bfloat16 [4096, 4096], P('row', 'col'), may hold values from -6 to 6
- left_basis: bfloat16 [4096, 4096], P('col', 'row'), may hold values from -0.09375 to 0.09375
- right_basis: bfloat16 [4096, 4096], P('row', 'col'), may hold values from -0.09375 to 0.09375
- first_moment: float32 [4096, 4096], P('row', 'col'), may hold values from -1.8 to 1.8
- second_moment: float32 [4096, 4096], P('row', 'col'), may hold values from 0.05 to 2
- weight: float32 [4096, 4096], P('row', 'col'), may hold values from -0.18 to 0.18
Outputs:
- new_weight: float32 [4096, 4096], P('row', 'col')
- update: bfloat16 [4096, 4096], P('row', 'col')
- new_first: float32 [4096, 4096], P('row', 'col')
- new_second: float32 [4096, 4096], P('row', 'col')
All inputs are finite; a program needn't handle non-finite values.
Results may differ from a plain program's by a relative error of at most 0.034.
Values may be sent and summed in bfloat16 or wider, within the bound.
A program may use at most 64 MiB of HBM per device.

v0:
```python
import jax
import jax.numpy as jnp
from jax import lax
from jax.sharding import PartitionSpec as P

beta_one = 0.9
beta_two = 0.95
epsilon = 1e-08
learn_rate = 0.0003
weight_decay = 0.1
step_count = 20.0


def contract_first(left, right):
    return lax.dot_general(
        left, right, (((0,), (0,)), ((), ())), preferred_element_type=jnp.float32
    )


def contract_last(left, right):
    return lax.dot_general(
        left, right, (((1,), (1,)), ((), ())), preferred_element_type=jnp.float32
    )


def on_device(gradient, left_basis, right_basis, first_moment, second_moment, weight):
    grad_panel = lax.all_gather(gradient, "row", axis=0, tiled=True)
    half_float = contract_first(lax.all_gather(left_basis, "col", axis=0, tiled=True), grad_panel)
    half_rotated = half_float.astype(jnp.bfloat16)
    half_row = lax.all_gather(half_rotated, "col", axis=1, tiled=True)
    rotated = jnp.dot(
        half_row,
        lax.all_gather(right_basis, "row", axis=0, tiled=True),
        preferred_element_type=jnp.float32,
    )
    new_first = beta_one * first_moment + (1.0 - beta_one) * rotated
    new_second = beta_two * second_moment + (1.0 - beta_two) * rotated * rotated
    first_hat = new_first / (1.0 - beta_one**step_count)
    second_hat = new_second / (1.0 - beta_two**step_count)
    normed = (first_hat / (jnp.sqrt(second_hat) + epsilon)).astype(jnp.bfloat16)
    partial_back = contract_last(normed, lax.all_gather(right_basis, "row", axis=0, tiled=True))
    back_half = lax.psum_scatter(
        partial_back.astype(jnp.bfloat16), "col", scatter_dimension=1, tiled=True
    )
    terms = jnp.dot(
        lax.all_gather(left_basis, "col", axis=0, tiled=True),
        back_half,
        preferred_element_type=jnp.float32,
    )
    full_update = lax.psum_scatter(
        terms.astype(jnp.bfloat16), "row", scatter_dimension=0, tiled=True
    ).astype(jnp.float32)
    update = full_update.astype(jnp.bfloat16)
    new_weight = weight - learn_rate * (full_update + weight_decay * weight)
    return (new_weight, update, new_first, new_second)


def solution(mesh):
    in_specs = (
        P("row", "col"),
        P("col", "row"),
        P("row", "col"),
        P("row", "col"),
        P("row", "col"),
        P("row", "col"),
    )
    out_specs = (P("row", "col"), P("row", "col"), P("row", "col"), P("row", "col"))
    return jax.shard_map(
        on_device, mesh=mesh, in_specs=in_specs, out_specs=out_specs, check_vma=False
    )
```

profile of v0, /device:TPU:24, one launch (start us, length us, event | category | flops | bytes accessed | tf_op | source)
XLA Modules:
  0.0 632.1 jit_solution(3189945040408121291)
XLA Ops:
  7.2 0.0 copy-start.5
  7.2 0.0 copy-start.4
  7.2 0.0 all-gather.7.cloned.1.call-start
  7.2 0.7 all-gather.7.cloned.1.call-update
  7.9 0.0 all-gather.5.cloned.1.call-start
  8.0 0.7 all-gather.5.cloned.1.call-update
  8.7 0.0 all-gather.11.cloned.1.call-start
  8.7 0.7 all-gather.11.cloned.1.call-update
  9.4 0.0 all-gather.9.cloned.1.call-start
  9.4 65.9 %all-gather.7.cloned.1.call-done = bf16[4096,128]{1,0:T(8,128)(2,1)} async-done(((bf16[256,128]{1,0:T(8,128)(2,1)}), bf16[4096,128]{1,0:T(8,128)(2,1)}) %all-gather.7.cloned.1.call-update) | async-done | bytes 1048592 | tf_op jit(solution)/shard_map/all_gather | solution.py:27
  75.3 134.9 %all-gather.5.cloned.1.call-done = bf16[4096,256]{1,0:T(8,128)(2,1)} async-done(((bf16[128,256]{1,0:T(8,128)(2,1)}), bf16[4096,256]{1,0:T(8,128)(2,1)}) %all-gather.5.cloned.1.call-update) | async-done | bytes 2097168 | tf_op jit(solution)/shard_map/all_gather | solution.py:46
  210.3 3.2 convolution_convert_fusion.2
  213.5 0.0 all-gather.9.cloned.1.call-update
  213.5 0.0 reduce-scatter.7.cloned.1.call-start
  213.6 53.1 %all-gather.11.cloned.1.call-done = bf16[4096,128]{1,0:T(8,128)(2,1)} async-done(((bf16[256,128]{1,0:T(8,128)(2,1)}), bf16[4096,128]{1,0:T(8,128)(2,1)}) %all-gather.11.cloned.1.call-update) | async-done | bytes 1048592 | tf_op jit(solution)/shard_map/all_gather | solution.py:33
  266.7 0.0 copy-start.1
  266.7 129.8 %all-gather.9.cloned.1.call-done = bf16[256,4096]{1,0:T(8,128)(2,1)} async-done(((bf16[256,128]{1,0:T(8,128)(2,1)}), bf16[256,4096]{1,0:T(8,128)(2,1)}) %all-gather.9.cloned.1.call-update) | async-done | bytes 2097168 | tf_op jit(solution)/shard_map/all_gather | solution.py:30
  396.6 0.0 copy-done.5
  396.6 0.0 copy-done.4
  396.6 2.6 multiply_add_fusion
  399.1 0.0 copy-start.2
  399.1 0.0 copy-start.3
  399.2 0.0 copy-done.1
  399.2 0.7 convolution_convert_fusion
  399.9 2.5 copy.13
  402.4 0.0 copy-done.2
  402.4 0.0 copy-done.3
  402.4 0.0 copy-start
  402.4 0.0 reduce-scatter.7.cloned.1.call-update
  402.4 0.0 copy-start.6
  402.4 0.0 reduce-scatter.5.cloned.1.call-start
  402.4 134.8 %reduce-scatter.7.cloned.1.call-done = bf16[128,256]{1,0:T(8,128)(2,1)} async-done(((bf16[4096,256]{1,0:T(8,128)(2,1)}), bf16[128,256]{1,0:T(8,128)(2,1)}) %reduce-scatter.7.cloned.1.call-update) | async-done | bytes 65552
  537.2 0.0 copy-done
  537.2 2.5 fusion
  539.8 0.0 reduce-scatter.5.cloned.1.call-update
  539.8 83.9 %reduce-scatter.5.cloned.1.call-done = bf16[256,128]{1,0:T(8,128)(2,1)} async-done(((bf16[4096,128]{1,0:T(8,128)(2,1)}), bf16[256,128]{1,0:T(8,128)(2,1)}) %reduce-scatter.5.cloned.1.call-update) | async-done | bytes 65552 | tf_op jit(solution)/shard_map/reduce_scatter | solution.py:50
  623.7 0.0 copy-done.6
  623.7 1.5 multiply_subtract_fusion
Async XLA Ops:
  7.2 389.4 %copy-start.5 = (f32[256,128]{1,0:T(8,128)S(1)}, f32[256,128]{1,0:T(8,128)}, u32[]{:S(2)}) copy-start(f32[256,128]{1,0:T(8,128)} %param.10) | copy-start | bytes 393220
  7.2 389.4 %copy-start.4 = (f32[256,128]{1,0:T(8,128)S(1)}, f32[256,128]{1,0:T(8,128)}, u32[]{:S(2)}) copy-start(f32[256,128]{1,0:T(8,128)} %param.9) | copy-start | bytes 393220
  7.2 68.1 %all-gather.7.cloned.1.call-start = ((), (), s32[]{:S(2)}) async-start(), calls=%async_computation.3 | async-start | bytes 1114112 | tf_op jit(solution)/shard_map/all_gather | solution.py:27
  7.9 202.3 %all-gather.5.cloned.1.call-start = ((), (), s32[]{:S(2)}) async-start(), calls=%async_computation.2 | async-start | bytes 2162688 | tf_op jit(solution)/shard_map/all_gather | solution.py:46
  8.7 258.1 %all-gather.11.cloned.1.call-start = ((), (), s32[]{:S(2)}) async-start(), calls=%async_computation.5 | async-start | bytes 1114112 | tf_op jit(solution)/shard_map/all_gather | solution.py:33
  9.4 387.2 %all-gather.9.cloned.1.call-start = ((), (), s32[]{:S(2)}) async-start(), calls=%async_computation.4 | async-start | bytes 2162688 | tf_op jit(solution)/shard_map/all_gather | solution.py:30
  213.5 323.7 %reduce-scatter.7.cloned.1.call-start = ((), (), s32[]{:S(2)}) async-start(), calls=%async_computation.7 | async-start | bytes 2162688
  266.7 132.4 %copy-start.1 = (bf16[4096,128]{1,0:T(8,128)(2,1)S(1)}, bf16[4096,128]{1,0:T(8,128)(2,1)}, u32[]{:S(2)}) copy-start(bf16[4096,128]{1,0:T(8,128)(2,1)} %all-gather.11.cloned.1.call-done) | copy-start | bytes 3145732
  399.1 3.2 copy-start.2
  399.1 3.2 copy-start.3
  402.4 134.9 %copy-start = (bf16[4096,256]{1,0:T(8,128)(2,1)S(1)}, bf16[4096,256]{1,0:T(8,128)(2,1)}, u32[]{:S(2)}) copy-start(bf16[4096,256]{1,0:T(8,128)(2,1)} %all-gather.5.cloned.1.call-done) | copy-start | bytes 6291460
  402.4 221.3 %copy-start.6 = (f32[256,128]{1,0:T(8,128)S(1)}, f32[256,128]{1,0:T(8,128)}, u32[]{:S(2)}) copy-start(f32[256,128]{1,0:T(8,128)} %param.11) | copy-start | bytes 393220
  402.4 221.3 %reduce-scatter.5.cloned.1.call-start = ((), (), s32[]{:S(2)}) async-start(), calls=%async_computation.6 | async-start | bytes 1114112 | tf_op jit(solution)/shard_map/reduce_scatter | solution.py:50
Sparse Core Ops, SparseCore 0:
  11.4 63.9 all-gather.6
  77.4 132.8 all-gather.4
  213.6 53.0 all-gather.10
  269.2 127.3 all-gather.8
  402.5 134.6 reduce-scatter.6
  543.0 80.6 reduce-scatter.4
where the time goes:
time: 632 us
  waiting for transfers between devices  605 us (96%)
  between operations  14.2 us (2%)
  matrix products  9.04 us (1%)
    unnamed x7, waiting for transfers between devices  137 us
    all_gather x1, waiting for transfers between devices, on_device(): lax.all_gather(left_basis, 'col', axis=0, tiled=True)  135 us
    all_gather x1, waiting for transfers between devices, on_device(): half_row = lax.all_gather(half_rotated, 'col', axis=1, tiled=True)  130 us
    reduce_scatter x1, waiting for transfers between devices, on_device(): lax.psum_scatter(terms.astype(jnp.bfloat16), 'row', scatter_dimension=0,...  83.9 us
    all_gather x1, waiting for transfers between devices, on_device(): grad_panel = lax.all_gather(gradient, 'row', axis=0, tiled=True)  65.9 us
    all_gather x1, waiting for transfers between devices, on_device(): lax.all_gather(right_basis, 'row', axis=0, tiled=True)  53.1 us
  transfers between devices with their start and end apart: 6, of which 6 were waited for; matrix products, arithmetic and copies ran while one was open for 1% of the time, Pallas kernels for 0%

commit v1 on v0

v1 whole, which is shorter than its diff:
```python
import functools

import jax
import jax.numpy as jnp
from jax import lax
from jax.experimental import pallas as pl
from jax.experimental.pallas import tpu as pltpu
from jax.sharding import PartitionSpec as P

beta_one = 0.9
beta_two = 0.95
epsilon = 1e-08
learn_rate = 0.0003
weight_decay = 0.1
step_count = 20.0

MESH = pl.DeviceIdType.MESH
CHUNKS = 2


def dot(left, right, left_dim, right_dim):
    return lax.dot_general(
        left,
        right,
        (((left_dim,), (right_dim,)), ((), ())),
        preferred_element_type=jnp.float32,
    )


def kernel(
    ny, nz, tr, tc,
    g_ref, l_ref, r_ref, m1_ref, m2_ref, w_ref,
    nw_ref, up_ref, nf_ref, ns_ref,
    gbuf, lbuf, lsib, rbuf, pbuf, ptile, xsend, xrecv, nbuf, qsend, qrecv, qfull,
    us_up, ur_up, us_dn, ur_dn,
    g_us, g_ur, g_ds, g_dr, l_us, l_ur, l_ds, l_dr, u_us, u_ur, u_ds, u_dr,
    rs_sem, rr_sem, rsib_s, rsib_r, ps_sem, pr_sem, psib_s, psib_r,
    qs_sem, qr_sem, lsib_s, lsib_r, x_s, x_r, n_s, n_r,
):
    bf16 = jnp.bfloat16
    ratio = tr // tc
    steps_up, steps_dn = nz // 2, nz - 1 - nz // 2
    row, col = lax.axis_index("row"), lax.axis_index("col")
    x_hi, y, c = lax.div(row, 2 * ny), lax.rem(lax.div(row, 2), ny), lax.rem(row, 2)
    x_lo, z = lax.div(col, nz), lax.rem(col, nz)
    sib = 1 - c
    diagonal = x_hi == x_lo

    def device(x_hi, y, c, x_lo, z):
        return ((x_hi * ny + y) * 2 + c, x_lo * nz + z)

    above = device(x_hi, y, c, x_lo, lax.rem(z + 1, nz))
    below = device(x_hi, y, c, x_lo, lax.rem(z + nz - 1, nz))
    sibling = device(x_hi, y, sib, x_lo, z)
    beside = device(x_hi, y, c, 1 - x_lo, z)
    beside_sib = device(x_hi, y, sib, 1 - x_lo, z)

    def copy(src, dst, send, recv, to):
        return pltpu.make_async_remote_copy(
            src_ref=src, dst_ref=dst, send_sem=send, recv_sem=recv,
            device_id=to, device_id_type=MESH,
        )

    def loop(n, body):
        lax.fori_loop(0, n, lambda i, carry: (body(i), carry)[1], 0)

    barrier = pltpu.get_barrier_semaphore()

    def greet(to):
        pl.semaphore_signal(barrier, inc=1, device_id=to, device_id_type=MESH)

    def greet_plane(i):
        peer_x, peer_y = lax.div(i, ny), lax.rem(i, ny)
        hi, lo = lax.div(peer_x, 2), lax.rem(peer_x, 2)
        pl.when(~((hi == x_hi) & (lo == x_lo) & (peer_y == y)))(
            lambda: greet(device(hi, peer_y, c, lo, z))
        )

    for to in (above, below, sibling, beside_sib):
        greet(to)
    loop(4 * ny, greet_plane)
    pl.semaphore_wait(barrier, 4 * ny - 1 + 4)

    def ring(buf, us, ur, ds, dr):
        rows = buf.shape[1] // CHUNKS

        def part(tile, ch):
            return buf.at[tile, pl.ds(ch * rows, rows)]

        def up(s, ch, sent):
            tile = lax.rem(z - s + 2 * nz - (0 if sent else 1), nz)
            return copy(part(tile, ch), part(tile, ch), us.at[ch, s], ur.at[ch, s], above)

        def down(s, ch, sent):
            tile = lax.rem(z + s + (0 if sent else 1), nz)
            return copy(part(tile, ch), part(tile, ch), ds.at[ch, s], dr.at[ch, s], below)

        def start():
            for ch in range(CHUNKS):
                up(0, ch, True).start()
                down(0, ch, True).start()

        def middle(s):
            for ch in range(CHUNKS):
                up(s - 1, ch, False).wait_recv()
                up(s, ch, True).start()
                down(s - 1, ch, False).wait_recv()
                down(s, ch, True).start()

        def last():
            for ch in range(CHUNKS):
                up(steps_up - 2, ch, False).wait_recv()
                up(steps_up - 1, ch, True).start()

        def finish():
            for ch in range(CHUNKS):
                down(steps_dn - 1, ch, False).wait_recv()
            for ch in range(CHUNKS):
                up(steps_up - 1, ch, False).wait_recv()

        def sent():
            def one(s):
                for ch in range(CHUNKS):
                    up(s, ch, True).wait_send()

            def two(s):
                for ch in range(CHUNKS):
                    down(s, ch, True).wait_send()

            loop(steps_up, one)
            loop(steps_dn, two)

        return start, middle, last, finish, sent

    def plane(buf, tile, ss, rs, sib_s, sib_r):
        mine = buf.at[x_lo, y * 2 + c]

        def out(i):
            hi, dy = lax.div(i, ny), lax.rem(i, ny)
            is_self = diagonal & (hi == x_hi) & (dy == 0)
            to = device(hi, lax.rem(y + dy, ny), c, x_hi, z)
            return is_self, copy(tile, mine, ss.at[hi, dy], rs.at[x_lo, y], to)

        def start():
            def one(i):
                is_self, send = out(i)
                pl.when(~is_self)(send.start)

            loop(2 * ny, one)

            @pl.when(diagonal)
            def _():
                mine[...] = tile[...]

        def forward(i, own):
            jj, ys = lax.div(i, ny), lax.rem(i, ny)
            slot = buf.at[jj, ys * 2 + (c if own else sib)]
            return jj, ys, slot, copy(slot, slot, sib_s.at[jj, ys], sib_r.at[jj, ys], sibling)

        def relay():
            def one(i):
                jj, ys, slot, send = forward(i, True)
                is_self = diagonal & (jj == x_lo) & (ys == y)
                pl.when(~is_self)(
                    copy(tile, slot, ss.at[0, 0], rs.at[jj, ys], sibling).wait_recv
                )
                send.start()

            loop(2 * ny, one)

        def finish():
            loop(2 * ny, lambda i: forward(i, False)[3].wait_recv())

        def sent():
            def one(i):
                is_self, send = out(i)
                pl.when(~is_self)(send.wait_send)
                forward(i, True)[3].wait_send()

            loop(2 * ny, one)

        return start, relay, finish, sent

    g_start, g_middle, g_last, g_finish, g_sent = ring(gbuf, g_us, g_ur, g_ds, g_dr)
    l_start, l_middle, l_last, l_finish, l_sent = ring(lbuf, l_us, l_ur, l_ds, l_dr)
    r_start, r_relay, r_finish, r_sent = plane(rbuf, r_ref, rs_sem, rr_sem, rsib_s, rsib_r)
    p_start, p_relay, p_finish, p_sent = plane(pbuf, ptile, ps_sem, pr_sem, psib_s, psib_r)

    def swap_start(which, partial):
        first, second = partial[:, :tc], partial[:, tc:]
        xsend[which] = jnp.where(x_lo == 0, second, first).astype(bf16)
        swap(which).start()
        return jnp.where(x_lo == 0, first, second)

    def swap(which):
        return copy(xsend.at[which], xrecv.at[which], x_s.at[which], x_r.at[which], beside)

    gbuf[z] = g_ref[...]
    lbuf[z] = l_ref[...]
    g_start()
    r_start()
    lax.fori_loop(1, steps_up // 2, lambda s, carry: (g_middle(s), carry)[1], 0)
    r_relay()
    lax.fori_loop(steps_up // 2, steps_dn, lambda s, carry: (g_middle(s), carry)[1], 0)
    g_last()
    l_start()
    r_finish()
    g_finish()

    partial = jnp.zeros((tr, 2 * tc), jnp.float32)
    for b in range(2 * ny):
        left = jnp.concatenate([gbuf[b * ratio + k] for k in range(ratio)], axis=1)
        right = jnp.concatenate([rbuf[0, b], rbuf[1, b]], axis=1)
        partial += dot(left, right, 1, 0)
    mine = swap_start(0, partial)
    ptile_f32 = mine
    if steps_dn > 1:
        l_middle(1)
    swap(0).wait_recv()
    ptile[...] = (ptile_f32 + xrecv[0].astype(jnp.float32)).astype(bf16)
    p_start()
    lax.fori_loop(2, steps_dn, lambda s, carry: (l_middle(s), carry)[1], 0)
    l_last()
    p_relay()
    l_finish()

    def share_l(yy):
        rows = pl.ds((2 * yy + sib) * ratio, ratio)
        return copy(lbuf.at[rows], lsib.at[yy], lsib_s.at[yy], lsib_r.at[yy], sibling)

    loop(ny, lambda yy: share_l(yy).start())
    p_finish()

    partial = jnp.zeros((tr, 2 * tc), jnp.float32)
    for b in range(2 * ny):
        left = lbuf[b * ratio : (b + 1) * ratio].reshape(tr, tr)
        right = jnp.concatenate([pbuf[0, b], pbuf[1, b]], axis=1)
        partial += dot(left, right, 0, 0)
    mine = swap_start(1, partial)
    swap(1).wait_recv()
    rotated = mine + xrecv[1].astype(jnp.float32)
    new_first = beta_one * m1_ref[...] + (1.0 - beta_one) * rotated
    new_second = beta_two * m2_ref[...] + (1.0 - beta_two) * rotated * rotated
    nf_ref[...] = new_first
    ns_ref[...] = new_second
    first_hat = new_first / (1.0 - beta_one**step_count)
    second_hat = new_second / (1.0 - beta_two**step_count)
    nbuf[c, x_lo] = (first_hat / (jnp.sqrt(second_hat) + epsilon)).astype(bf16)

    def share_n(k, to, core, lo):
        slot = nbuf.at[core, lo]
        return copy(nbuf.at[c, x_lo], slot, n_s.at[k], n_r.at[k], to)

    targets = (beside, sibling, beside_sib)
    sources = ((c, 1 - x_lo), (sib, x_lo), (sib, 1 - x_lo))
    for k in range(3):
        share_n(k, targets[k], c, x_lo).start()
    loop(ny, lambda yy: share_l(yy).wait_recv())
    for k in range(3):
        share_n(k, targets[k], *sources[k]).wait_recv()

    def q_out(yy, jj):
        is_self = diagonal & (jj == x_lo) & (yy == y)
        to = device(x_lo, yy, c, jj, z)
        return is_self, copy(
            qsend.at[jj, yy], qrecv.at[x_hi, y], qs_sem.at[jj, yy], qr_sem.at[x_hi, y], to
        )

    own_n = jnp.concatenate([nbuf[c, 0], nbuf[c, 1]], axis=1)
    sib_n = jnp.concatenate([nbuf[sib, 0], nbuf[sib, 1]], axis=1)
    for yy in range(ny):
        own_l = lbuf[pl.ds((2 * yy + c) * ratio, ratio)].reshape(tr, tr)
        sib_l = lsib[yy].reshape(tr, tr)
        block = (dot(own_l, own_n, 1, 0) + dot(sib_l, sib_n, 1, 0)).astype(bf16)
        for jj in range(2):
            qsend[jj, yy] = block[:, jj * tc : (jj + 1) * tc]
            is_self, send = q_out(yy, jj)
            pl.when(~is_self)(send.start)

    @pl.when(diagonal)
    def _():
        qrecv[x_hi, y] = qsend[x_lo, y]

    total = jnp.zeros((tr, tc), jnp.float32)
    for hi in range(2):
        for yy in range(ny):
            is_self = diagonal & (hi == x_hi) & (yy == y)
            pl.when(~is_self)(
                copy(ptile, qrecv.at[hi, yy], qs_sem.at[0, 0], qr_sem.at[hi, yy], beside).wait_recv
            )
            total += qrecv[hi, yy].astype(jnp.float32)
    qfull[x_lo] = total.astype(bf16)

    def share_q(lo):
        return copy(qfull.at[x_lo], qfull.at[lo], x_s.at[2], x_r.at[2], beside)

    share_q(x_lo).start()
    share_q(1 - x_lo).wait_recv()

    def tile_of(d):
        d = lax.rem(d + 2 * nz, nz)
        rows = pl.ds(lax.rem(d, ratio) * tc, tc)
        at = lax.div(d, ratio)
        left = jnp.concatenate([qfull[0], qfull[1]], axis=1)
        right = jnp.concatenate([rbuf[0, at, rows], rbuf[1, at, rows]], axis=1)
        return dot(left, right, 1, 1)

    def u_up(s):
        return copy(us_up.at[s], ur_up.at[s], u_us.at[s], u_ur.at[s], above)

    def u_down(s):
        return copy(us_dn.at[s], ur_dn.at[s], u_ds.at[s], u_dr.at[s], below)

    us_up[0] = tile_of(z + steps_up).astype(bf16)
    u_up(0).start()
    us_dn[0] = tile_of(z - steps_dn).astype(bf16)
    u_down(0).start()

    def up_step(s):
        term = tile_of(z + steps_up - s)
        u_up(s - 1).wait_recv()
        us_up[s] = (term + ur_up[s - 1].astype(jnp.float32)).astype(bf16)
        u_up(s).start()

    def u_step(s):
        up_step(s)
        term = tile_of(z - steps_dn + s)
        u_down(s - 1).wait_recv()
        us_dn[s] = (term + ur_dn[s - 1].astype(jnp.float32)).astype(bf16)
        u_down(s).start()

    lax.fori_loop(1, steps_dn, lambda s, carry: (u_step(s), carry)[1], 0)
    up_step(steps_up - 1)
    full = tile_of(z)
    u_down(steps_dn - 1).wait_recv()
    full += ur_dn[steps_dn - 1].astype(jnp.float32)
    u_up(steps_up - 1).wait_recv()
    full += ur_up[steps_up - 1].astype(jnp.float32)
    weight = w_ref[...]
    up_ref[...] = full.astype(bf16)
    nw_ref[...] = weight - learn_rate * (full + weight_decay * weight)

    g_sent()
    l_sent()
    r_sent()
    p_sent()
    for which in range(2):
        swap(which).wait_send()
    share_q(x_lo).wait_send()
    loop(ny, lambda yy: share_l(yy).wait_send())
    for k in range(3):
        share_n(k, targets[k], c, x_lo).wait_send()

    def q_sent(i):
        is_self, send = q_out(lax.rem(i, ny), lax.div(i, ny))
        pl.when(~is_self)(send.wait_send)

    loop(2 * ny, q_sent)
    loop(steps_up, lambda s: u_up(s).wait_send())
    loop(steps_dn, lambda s: u_down(s).wait_send())


def on_device(n_row, n_col, gradient, left_basis, right_basis, first_moment, second_moment, weight):
    ny, nz = n_row // 4, n_col // 2
    tr, tc = gradient.shape
    up, dn = nz // 2, nz - 1 - nz // 2
    bf16 = jnp.bfloat16
    ratio = tr // tc
    dma = pltpu.SemaphoreType.DMA
    ring = [dma((CHUNKS, up)), dma((CHUNKS, up)), dma((CHUNKS, dn)), dma((CHUNKS, dn))]
    f32_tile = jax.ShapeDtypeStruct((tr, tc), jnp.float32)
    vmem = pl.BlockSpec(memory_space=pltpu.VMEM)
    return pl.pallas_call(
        functools.partial(kernel, ny, nz, tr, tc),
        out_shape=[f32_tile, jax.ShapeDtypeStruct((tr, tc), bf16), f32_tile, f32_tile],
        in_specs=[vmem] * 6,
        out_specs=[vmem] * 4,
        scratch_shapes=[
            pltpu.VMEM((nz, tr, tc), bf16),
            pltpu.VMEM((nz, tc, tr), bf16),
            pltpu.VMEM((ny, ratio, tc, tr), bf16),
            pltpu.VMEM((2, 2 * ny, tr, tc), bf16),
            pltpu.VMEM((2, 2 * ny, tr, tc), bf16),
            pltpu.VMEM((tr, tc), bf16),
            pltpu.VMEM((2, tr, tc), bf16),
            pltpu.VMEM((2, tr, tc), bf16),
            pltpu.VMEM((2, 2, tr, tc), bf16),
            pltpu.VMEM((2, ny, tr, tc), bf16),
            pltpu.VMEM((2, ny, tr, tc), bf16),
            pltpu.VMEM((2, tr, tc), bf16),
            pltpu.VMEM((up, tr, tc), bf16),
            pltpu.VMEM((up, tr, tc), bf16),
            pltpu.VMEM((dn, tr, tc), bf16),
            pltpu.VMEM((dn, tr, tc), bf16),
        ]
        + ring
        + ring
        + [dma((up,)), dma((up,)), dma((dn,)), dma((dn,))]
        + [dma((2, ny))] * 10
        + [dma((ny,)), dma((ny,)), dma((3,)), dma((3,)), dma((3,)), dma((3,))],
        compiler_params=pltpu.CompilerParams(
            collective_id=0, has_side_effects=True, vmem_limit_bytes=40 * 2**20
        ),
    )(gradient, left_basis, right_basis, first_moment, second_moment, weight)


def solution(mesh):
    spec = P("row", "col")
    return jax.shard_map(
        functools.partial(on_device, mesh.shape["row"], mesh.shape["col"]),
        mesh=mesh,
        in_specs=(spec, P("col", "row"), spec, spec, spec, spec),
        out_specs=(spec,) * 4,
        check_vma=False,
    )
```

time: 632 us -> 130 us (0.21)
  waiting for transfers between devices: 605 us -> 0 us
  Pallas kernels: 0 us -> 121 us
  between operations: 14.2 us -> 0.66 us
  matrix products: 9.04 us -> 0 us
    all_gather x4 -> x0, waiting for transfers between devices: 384 us -> none  [the longest x1 135 us: on_device(): lax.all_gather(left_basis, 'col', axis=0, tiled=True)]
    unnamed x7 -> x0, waiting for transfers between devices: 137 us -> none
    pallas_call x0 -> x1, Pallas kernels: none -> 121 us  [on_device(): pl.pallas_call(functools.partial(kernel, ny, nz, tr, tc), out_shape=[f32_...]
    reduce_scatter x1 -> x0, waiting for transfers between devices: 83.9 us -> none  [on_device(): lax.psum_scatter(terms.astype(jnp.bfloat16), 'row', scatter_dimension=0,...]
    dot_general x4 -> x0, matrix products: 9.04 us -> none  [the longest x1 3.24 us: contract_first(): lax.dot_general(left, right, (((0,), (0,)), ((), ())), preferred_element_...]
  transfers between devices with their start and end apart: 6 -> 0, of which waited for: 6 -> 0; matrix products, arithmetic and copies ran while one was open for 1% -> 0% of each run, Pallas kernels for 0% -> 0%
where the time goes in v1:
time: 130 us; the launch traced here: 129 us
  Pallas kernels  121 us (93%)
  local copies, waits for them, and re-layouts  7.82 us (6%)
    pallas_call x1, Pallas kernels, on_device(): pl.pallas_call(functools.partial(kernel, ny, nz, tr, tc), out_shape=[f32_...  121 us
    unnamed x16, local copies, waits for them, and re-layouts  7.82 us

profile of v1, /device:TPU:24, one launch (start us, length us, event | category | flops | bytes accessed | tf_op | source)
XLA Modules:
  0.0 129.3 jit_solution(12950723693772833543)
XLA Ops:
  0.6 0.0 copy-start
  0.6 0.9 copy-done
  1.5 0.0 copy-start.1
  1.5 0.9 copy-done.1
  2.4 0.0 copy-start.2
  2.4 0.9 copy-done.2
  3.3 0.0 copy-start.3
  3.3 0.8 copy-done.3
  4.2 0.0 copy-start.4
  4.2 0.8 copy-done.4
  5.0 0.0 copy-start.5
  5.0 0.8 copy-done.5
  5.9 120.8 %shard_map.93 = (f32[256,128]{1,0:T(8,128)S(1)}, bf16[256,128]{1,0:T(8,128)(2,1)S(1)}, f32[256,128]{1,0:T(8,128)S(1)}, f32[256,128]{1,0:T(8,128)S(1)}) custom-call(bf16[256,128]{1,0:T(8,128)(2,1)S(1)} %copy-done.3, bf16[128,256]{1,0:T(8,128)(2,1)S(1)} %copy-done.4, bf16[256,128]{1,0:T(8,128)(2,1)S(1)} %copy-done.5, f32[256,128]{1,0:T(8,128)S(1)} %copy-done, ...), custom_call_target="tpu_custom_call" | custom-call | tf_op jit(solution)/shard_map/pallas_call | solution.py:373
  126.7 0.7 copy.14
  127.4 0.6 copy.15
  128.0 0.7 copy.16
  128.7 0.7 copy.17
Async XLA Ops:
  0.6 0.9 copy-start
  1.5 0.9 copy-start.1
  2.4 0.9 copy-start.2
  3.3 0.8 copy-start.3
  4.2 0.8 copy-start.4
  5.0 0.8 copy-start.5

commit v2 on v0

v2 whole, which is shorter than its diff:
```python
import functools

import jax
import jax.numpy as jnp
from jax import lax
from jax.experimental import pallas as pl
from jax.experimental.pallas import tpu as pltpu
from jax.sharding import PartitionSpec as P

beta_one = 0.9
beta_two = 0.95
epsilon = 1e-08
learn_rate = 0.0003
weight_decay = 0.1
step_count = 20.0

MESH = pl.DeviceIdType.MESH
G_HOP, L_HOP, U_HOP = 1, 1, 2
L_PARTS = 2


def dot(left, right, left_dim, right_dim):
    return lax.dot_general(
        left,
        right,
        (((left_dim,), (right_dim,)), ((), ())),
        preferred_element_type=jnp.float32,
    )


def loop(n, body):
    lax.fori_loop(0, n, lambda i, carry: (body(i), carry)[1], 0)


def copy(src, dst, send, recv, to):
    return pltpu.make_async_remote_copy(
        src_ref=src, dst_ref=dst, send_sem=send, recv_sem=recv,
        device_id=to, device_id_type=MESH,
    )


def hops(distance, hop):
    return [hop] * (distance // hop) + ([distance % hop] if distance % hop else [])


class Gather:
    def __init__(self, z, nz, sign, hop, distance, pieces, part, first, send, recv, at):
        self.z, self.nz, self.sign, self.pieces = z, nz, sign, pieces
        self.part, self.first, self.send, self.recv, self.at = part, first, send, recv, at
        self.hops = hops(distance, hop)
        self.stops = [sum(self.hops[:k]) for k in range(len(self.hops) + 1)]

    def piece(self, k, off, ch, sender):
        i = self.stops[k] + off - 1
        away = self.stops[k] + (0 if sender else off)
        tile = self.part(lax.rem(self.z - self.sign * away + 2 * self.nz, self.nz), ch)
        src, dst, other = tile, tile, False
        if k == 0 and sender:
            src, dst, other = self.first(ch)
        to = self.at(lax.rem(self.z + self.sign * off + self.nz, self.nz), other)
        return copy(src, dst, self.send.at[ch, i], self.recv.at[ch, i], to)

    def step(self, k, ch):
        if k < len(self.hops):
            if k > 0:
                self.piece(k - 1, self.hops[k - 1], ch, False).wait_recv()
            for off in range(self.hops[k], 0, -1):
                self.piece(k, off, ch, True).start()

    def finish(self):
        last = len(self.hops) - 1
        for k, hop in enumerate(self.hops):
            for off in range(1, hop + (k == last)):
                for ch in range(self.pieces):
                    self.piece(k, off, ch, False).wait_recv()

    def sent(self):
        for k, hop in enumerate(self.hops):
            for off in range(1, hop + 1):
                for ch in range(self.pieces):
                    self.piece(k, off, ch, True).wait_send()


class Scatter:
    def __init__(self, z, nz, sign, hop, distance, own, out, into, send, recv, at):
        self.z, self.nz, self.sign = z, nz, sign
        self.own, self.out, self.into, self.send, self.recv, self.at = own, out, into, send, recv, at
        self.hops = hops(distance, hop)
        self.stops = [sum(self.hops[:k]) for k in range(len(self.hops) + 1)]

    def piece(self, k, off, ch):
        i = self.stops[k] + off - 1
        to = self.at(lax.rem(self.z + self.sign * off + self.nz, self.nz), k == 0 and ch == 1)
        return copy(self.out.at[ch, i], self.into.at[ch, i], self.send.at[ch, i], self.recv.at[ch, i], to)

    def arrived(self, k, ch, total):
        if k < len(self.hops):
            for off in range(1, self.hops[k] + 1):
                self.piece(k, off, ch).wait_recv()
                total += self.into[ch, self.stops[k] + off - 1].astype(jnp.float32)
        return total

    def far(self, k, ch):
        if k < len(self.hops):
            stop = self.stops[k + 1]
            total = self.arrived(k + 1, ch, self.own(self.sign * stop, ch))
            self.out[ch, stop - 1] = total.astype(jnp.bfloat16)
            self.piece(k, self.hops[k], ch).start()

    def near(self, k, ch):
        if k < len(self.hops):
            for off in range(1, self.hops[k]):
                stop = self.stops[k] + off
                self.out[ch, stop - 1] = self.own(self.sign * stop, ch).astype(jnp.bfloat16)
                self.piece(k, off, ch).start()

    def sent(self):
        for k, hop in enumerate(self.hops):
            for off in range(1, hop + 1):
                for ch in range(2):
                    self.piece(k, off, ch).wait_send()


def kernel(
    ny, nz, tr, tc,
    g_hbm, l_hbm, r_hbm, m1_hbm, m2_hbm, w_hbm,
    nw_hbm, up_hbm, nf_hbm, ns_hbm,
    g_ref, m1_ref, m2_ref, w_ref, nw_ref, up_ref, nf_ref, ns_ref,
    gbuf, lbuf, lsib, rbuf, ptile, pbuf, xsend, xrecv, nbuf, qsend, qrecv,
    uo_up, ui_up, uo_dn, ui_dn, uo_x, ui_x,
    in_sem, out_sem,
    g_us, g_ur, g_ds, g_dr, l_us, l_ur, l_ds, l_dr, u_us, u_ur, u_ds, u_dr,
    r_s, r_r, rsib_s, rsib_r, p_s, p_r, psib_s, psib_r, q_s, q_r,
    lsib_s, lsib_r, x_s, x_r, n_s, n_r,
):
    bf16 = jnp.bfloat16
    ratio, hr = tr // tc, tr // 2
    far_up, far_dn = nz // 2, nz - 1 - nz // 2
    row, col = lax.axis_index("row"), lax.axis_index("col")
    x_hi, y, c = lax.div(row, 2 * ny), lax.rem(lax.div(row, 2), ny), lax.rem(row, 2)
    x_lo, z = lax.div(col, nz), lax.rem(col, nz)
    sib = 1 - c
    diagonal = x_hi == x_lo

    own_r = rbuf.at[x_hi, x_lo, y * 2 + c]
    sources = (g_hbm, l_hbm, r_hbm, m1_hbm, m2_hbm, w_hbm)
    places = (g_ref, lbuf.at[z], own_r, m1_ref, m2_ref, w_ref)
    loads = [pltpu.make_async_copy(s, d, in_sem.at[i]) for i, (s, d) in enumerate(zip(sources, places))]
    for load in loads:
        load.start()

    def device(x_hi, y, c, x_lo, z):
        return ((x_hi * ny + y) * 2 + c, x_lo * nz + z)

    def along(to_z, other):
        return device(x_hi, y, c, 1 - x_lo if other else x_lo, to_z)

    sibling = device(x_hi, y, sib, x_lo, z)
    beside = device(x_hi, y, c, 1 - x_lo, z)
    beside_sib = device(x_hi, y, sib, 1 - x_lo, z)

    barrier = pltpu.get_barrier_semaphore()

    def greet(to):
        pl.semaphore_signal(barrier, inc=1, device_id=to, device_id_type=MESH)

    def in_plane(i):
        peer = lax.rem(x_hi * 2 + x_lo + lax.div(i, ny), 4)
        return lax.div(peer, 2), lax.rem(peer, 2), lax.rem(y + lax.rem(i, ny), ny)

    def greet_plane(i):
        hi, lo, yy = in_plane(i + 1)
        greet(device(hi, yy, c, lo, z))

    near = sorted({k % nz for k in (1, -1, 2, -2)} - {0})
    for k in near:
        for other in (False, True):
            greet(along(lax.rem(z + k, nz), other))
    greet(sibling)
    greet(beside_sib)
    loop(4 * ny - 1, greet_plane)
    pl.semaphore_wait(barrier, 2 * len(near) + 2 + 4 * ny - 1)

    def g_part(tile, ch):
        return gbuf.at[x_lo if ch == 0 else 1 - x_lo, tile]

    def g_half(which):
        return g_ref.at[pl.ds(pl.multiple_of(which * hr, hr), hr)]

    def g_first(ch):
        return g_half(x_lo if ch == 0 else 1 - x_lo), gbuf.at[x_lo, z], ch == 1

    lrows = tc // L_PARTS

    def l_part(tile, ch):
        return lbuf.at[tile, pl.ds(ch * lrows, lrows)]

    def l_first(ch):
        return l_part(z, ch), l_part(z, ch), False

    g_rings = [
        Gather(z, nz, 1, G_HOP, far_up, 2, g_part, g_first, g_us, g_ur, along),
        Gather(z, nz, -1, G_HOP, far_dn, 2, g_part, g_first, g_ds, g_dr, along),
    ]
    l_rings = [
        Gather(z, nz, 1, L_HOP, far_up, L_PARTS, l_part, l_first, l_us, l_ur, along),
        Gather(z, nz, -1, L_HOP, far_dn, L_PARTS, l_part, l_first, l_ds, l_dr, along),
    ]

    pending = [ring.sent for ring in g_rings + l_rings]

    def ring_step(rings, k):
        for ch in range(rings[0].pieces):
            for ring in rings:
                ring.step(k, ch)

    def g_beside():
        return copy(g_half(1 - x_lo), gbuf.at[x_lo, z], x_s.at[0], x_r.at[0], beside)

    def r_out(i):
        hi, lo, yy = in_plane(i)
        return copy(
            own_r, own_r, r_s.at[i], r_r.at[x_hi * 2 + x_lo, y], device(hi, yy, c, lo, z)
        )

    def r_relay(i, own):
        hi, lo, yy = in_plane(i)
        slot = rbuf.at[hi, lo, yy * 2 + (c if own else sib)]
        at = (hi * 2 + lo, yy)
        send = copy(slot, slot, rsib_s.at[at], rsib_r.at[at], sibling)
        arrive = copy(slot, slot, r_s.at[0], r_r.at[at], sibling)
        return arrive, send

    def r_pass(i):
        arrive, send = r_relay(i, True)
        arrive.wait_recv()
        send.start()

    loads[0].wait()
    g_ref_ready = pl.ds(pl.multiple_of(x_lo * hr, hr), hr)
    gbuf[x_lo, z] = g_ref[g_ref_ready, :]
    ring_step(g_rings, 0)
    g_beside().start()
    loads[1].wait()
    ring_step(l_rings, 0)
    loads[2].wait()
    loop(4 * ny - 1, lambda i: r_out(i + 1).start())
    r_relay(0, True)[1].start()

    pending.append(g_beside().wait_send)
    pending.append(lambda: loop(4 * ny - 1, lambda i: r_out(i + 1).wait_send()))
    pending.append(lambda: loop(4 * ny, lambda i: r_relay(i, True)[1].wait_send()))
    g_steps, l_steps = len(g_rings[0].hops), len(l_rings[0].hops)
    relayed, rounds = 1, max(g_steps, l_steps)
    for k in range(1, rounds):
        ring_step(g_rings, k)
        ring_step(l_rings, k)
        if k >= rounds // 2:
            left = rounds - k
            upto = relayed + (4 * ny - relayed + left - 1) // left
            lax.fori_loop(relayed, upto, lambda i, carry: (r_pass(i), carry)[1], 0)
            relayed = upto
    lax.fori_loop(relayed, 4 * ny, lambda i, carry: (r_pass(i), carry)[1], 0)
    loop(4 * ny, lambda i: r_relay(i, False)[1].wait_recv())
    for ring in g_rings:
        ring.finish()
    g_beside().wait_recv()

    partial = jnp.zeros((hr, 2 * tc), jnp.float32)
    for hi in range(2):
        for b in range(2 * ny):
            left = jnp.concatenate([gbuf[hi, b * ratio + k] for k in range(ratio)], axis=1)
            right = jnp.concatenate([rbuf[hi, 0, b], rbuf[hi, 1, b]], axis=1)
            partial += dot(left, right, 1, 0)
    ptile[...] = partial.astype(bf16)

    own_p = pbuf.at[y * 2 + c, x_lo]

    def p_out(i):
        hi, dy = lax.div(i, ny), lax.rem(i, ny)
        is_self = diagonal & (hi == x_hi) & (dy == 0)
        to = device(hi, lax.rem(y + dy, ny), c, x_hi, z)
        return is_self, copy(ptile, own_p, p_s.at[hi, dy], p_r.at[x_lo, y], to)

    def p_start(i):
        is_self, send = p_out(i)
        pl.when(~is_self)(send.start)

    loop(2 * ny, p_start)

    def p_sent(i):
        is_self, send = p_out(i)
        pl.when(~is_self)(send.wait_send)

    pending.append(lambda: loop(2 * ny, p_sent))

    @pl.when(diagonal)
    def _():
        pbuf[y * 2 + c, x_lo] = ptile[...]

    for ring in l_rings:
        ring.finish()

    def share_l(yy):
        rows = pl.ds((2 * yy + sib) * ratio, ratio)
        return copy(lbuf.at[rows], lsib.at[yy], lsib_s.at[yy], lsib_r.at[yy], sibling)

    def p_relay(dy, lo, own):
        yy = lax.rem(y + dy, ny)
        slot = pbuf.at[yy * 2 + (c if own else sib), lo]
        is_self = diagonal & (lo == x_lo) & (dy == 0)
        arrive = copy(ptile, slot, p_s.at[0, 0], p_r.at[lo, yy], sibling)
        return is_self, arrive, copy(slot, slot, psib_s.at[lo, yy], psib_r.at[lo, yy], sibling)

    partial = jnp.zeros((tr, 2 * tc), jnp.float32)

    def rotate(partial, dy, core):
        block = lax.rem(y + dy, ny) * 2 + core
        left = lbuf[pl.ds(block * ratio, ratio)].reshape(tr, tr)
        return partial + dot(left, pbuf[block].reshape(tr, 2 * tc), 0, 0)

    for dy in range(ny):
        for lo in range(2):
            is_self, arrive, send = p_relay(dy, lo, True)
            pl.when(~is_self)(arrive.wait_recv)
            send.start()
        partial = rotate(partial, dy, c)
    for dy in range(ny):
        for lo in range(2):
            p_relay(dy, lo, False)[2].wait_recv()
        partial = rotate(partial, dy, sib)

    pending.append(
        lambda: loop(2 * ny, lambda i: p_relay(lax.rem(i, ny), lax.div(i, ny), True)[2].wait_send())
    )
    first, second = partial[:, :tc], partial[:, tc:]
    xsend[...] = jnp.where(x_lo == 0, second, first).astype(bf16)
    swap = copy(xsend, xrecv, x_s.at[1], x_r.at[1], beside)
    swap.start()
    loop(ny, lambda yy: share_l(yy).start())
    for load in loads[3:]:
        load.wait()
    mine = jnp.where(x_lo == 0, first, second)
    swap.wait_recv()
    pending.append(swap.wait_send)
    pending.append(lambda: loop(ny, lambda yy: share_l(yy).wait_send()))
    rotated = mine + xrecv[...].astype(jnp.float32)
    new_first = beta_one * m1_ref[...] + (1.0 - beta_one) * rotated
    new_second = beta_two * m2_ref[...] + (1.0 - beta_two) * rotated * rotated
    first_hat = new_first / (1.0 - beta_one**step_count)
    second_hat = new_second / (1.0 - beta_two**step_count)
    nbuf[c, x_lo] = (first_hat / (jnp.sqrt(second_hat) + epsilon)).astype(bf16)

    def share_n(k, to, core, lo):
        slot = nbuf.at[core, lo]
        return copy(nbuf.at[c, x_lo], slot, n_s.at[k], n_r.at[k], to)

    targets = (beside, beside_sib, sibling)
    origins = ((c, 1 - x_lo), (sib, 1 - x_lo), (sib, x_lo))
    for k in range(3):
        share_n(k, targets[k], c, x_lo).start()
    nf_ref[...] = new_first
    ns_ref[...] = new_second
    saves = [
        pltpu.make_async_copy(s, d, out_sem.at[i])
        for i, (s, d) in enumerate(
            ((nf_ref, nf_hbm), (ns_ref, ns_hbm), (nw_ref, nw_hbm), (up_ref, up_hbm))
        )
    ]
    saves[0].start()
    saves[1].start()
    pending += [saves[0].wait, saves[1].wait]
    loop(ny, lambda yy: share_l(yy).wait_recv())
    for k in range(3):
        share_n(k, targets[k], *origins[k]).wait_recv()
        pending.append(share_n(k, targets[k], c, x_lo).wait_send)

    def q_out(dy, half):
        yy = lax.rem(y + dy, ny)
        is_self = diagonal & (half == x_lo) & (dy == 0)
        to = device(x_lo, yy, c, half, z)
        return is_self, copy(
            qsend.at[dy, half], qrecv.at[x_hi, y], q_s.at[dy, half], q_r.at[x_hi, y], to
        )

    own_n = jnp.concatenate([nbuf[c, 0], nbuf[c, 1]], axis=1)
    sib_n = jnp.concatenate([nbuf[sib, 0], nbuf[sib, 1]], axis=1)
    for step in range(ny):
        dy = (step + 1) % ny
        yy = lax.rem(y + dy, ny)
        own_l = lbuf[pl.ds((2 * yy + c) * ratio, ratio)].reshape(tr, tr)
        sib_l = lsib[yy].reshape(tr, tr)
        block = (dot(own_l, own_n, 1, 0) + dot(sib_l, sib_n, 1, 0)).astype(bf16)
        for half in range(2):
            qsend[dy, half] = block[half * hr : (half + 1) * hr]
            is_self, send = q_out(dy, half)
            pl.when(~is_self)(send.start)

    @pl.when(diagonal)
    def _():
        qrecv[x_hi, y] = qsend[0, x_lo]

    total = jnp.zeros((hr, 2 * tc), jnp.float32)
    for dy in range(ny):
        yy = lax.rem(y + dy, ny)
        for hi in range(2):
            is_self = diagonal & (hi == x_hi) & (dy == 0)
            arrive = copy(ptile, qrecv.at[hi, yy], q_s.at[0, 0], q_r.at[hi, yy], beside)
            pl.when(~is_self)(arrive.wait_recv)
            total += qrecv[hi, yy].astype(jnp.float32)
    q = total.astype(bf16)

    def q_sent(i):
        is_self, send = q_out(lax.rem(i, ny), lax.div(i, ny))
        pl.when(~is_self)(send.wait_send)

    pending.append(lambda: loop(2 * ny, q_sent))

    def u_own(away, ch):
        d = lax.rem(z + away + nz, nz)
        hi = x_lo if ch == 0 else 1 - x_lo
        rows = pl.ds(pl.multiple_of(lax.rem(d, ratio) * tc, tc), tc)
        at = lax.div(d, ratio)
        right = jnp.concatenate([rbuf[hi, 0, at, rows], rbuf[hi, 1, at, rows]], axis=1)
        return dot(q, right, 1, 1)

    u_rings = [
        Scatter(z, nz, 1, U_HOP, far_up, u_own, uo_up, ui_up, u_us, u_ur, along),
        Scatter(z, nz, -1, U_HOP, far_dn, u_own, uo_dn, ui_dn, u_ds, u_dr, along),
    ]
    u_beside = copy(uo_x, ui_x, x_s.at[2], x_r.at[2], beside)
    for k in reversed(range(len(u_rings[0].hops))):
        for ch in (1, 0):
            for ring in u_rings:
                ring.far(k, ch)
            for ring in u_rings:
                ring.near(k, ch)
        if k == len(u_rings[0].hops) - 1:
            uo_x[...] = u_own(0, 1).astype(bf16)
            u_beside.start()

    def finish(which, total, ch):
        for ring in u_rings:
            total = ring.arrived(0, ch, total)
        rows = pl.ds(pl.multiple_of(which * hr, hr), hr)
        weight = w_ref[rows, :]
        up_ref[rows, :] = total.astype(bf16)
        nw_ref[rows, :] = weight - learn_rate * (total + weight_decay * weight)

    mine = u_own(0, 0)
    u_beside.wait_recv()
    finish(1 - x_lo, ui_x[...].astype(jnp.float32), 1)
    finish(x_lo, mine, 0)
    saves[2].start()
    saves[3].start()
    pending += [saves[2].wait, saves[3].wait, u_beside.wait_send]
    pending += [ring.sent for ring in u_rings]

    for wait in pending:
        wait()


def on_device(n_row, n_col, gradient, left_basis, right_basis, first_moment, second_moment, weight):
    ny, nz = n_row // 4, n_col // 2
    tr, tc = gradient.shape
    up, dn = nz // 2, nz - 1 - nz // 2
    bf16, f32 = jnp.bfloat16, jnp.float32
    ratio, hr = tr // tc, tr // 2
    dma = pltpu.SemaphoreType.DMA
    f32_tile = jax.ShapeDtypeStruct((tr, tc), f32)
    anywhere = pl.BlockSpec(memory_space=pl.ANY)

    def ring(pieces):
        return [dma((pieces, up)), dma((pieces, up)), dma((pieces, dn)), dma((pieces, dn))]

    return pl.pallas_call(
        functools.partial(kernel, ny, nz, tr, tc),
        out_shape=[f32_tile, jax.ShapeDtypeStruct((tr, tc), bf16), f32_tile, f32_tile],
        in_specs=[anywhere] * 6,
        out_specs=[anywhere] * 4,
        scratch_shapes=[
            pltpu.VMEM((tr, tc), bf16),
            pltpu.VMEM((tr, tc), f32),
            pltpu.VMEM((tr, tc), f32),
            pltpu.VMEM((tr, tc), f32),
            pltpu.VMEM((tr, tc), f32),
            pltpu.VMEM((tr, tc), bf16),
            pltpu.VMEM((tr, tc), f32),
            pltpu.VMEM((tr, tc), f32),
            pltpu.VMEM((2, nz, hr, tc), bf16),
            pltpu.VMEM((nz, tc, tr), bf16),
            pltpu.VMEM((ny, ratio, tc, tr), bf16),
            pltpu.VMEM((2, 2, 2 * ny, tr, tc), bf16),
            pltpu.VMEM((hr, 2 * tc), bf16),
            pltpu.VMEM((2 * ny, 2, hr, 2 * tc), bf16),
            pltpu.VMEM((tr, tc), bf16),
            pltpu.VMEM((tr, tc), bf16),
            pltpu.VMEM((2, 2, tr, tc), bf16),
            pltpu.VMEM((ny, 2, hr, 2 * tc), bf16),
            pltpu.VMEM((2, ny, hr, 2 * tc), bf16),
            pltpu.VMEM((2, up, hr, tc), bf16),
            pltpu.VMEM((2, up, hr, tc), bf16),
            pltpu.VMEM((2, dn, hr, tc), bf16),
            pltpu.VMEM((2, dn, hr, tc), bf16),
            pltpu.VMEM((hr, tc), bf16),
            pltpu.VMEM((hr, tc), bf16),
            dma((6,)),
            dma((4,)),
        ]
        + ring(2)
        + ring(L_PARTS)
        + ring(2)
        + [dma((4 * ny,)), dma((4, ny)), dma((4, ny)), dma((4, ny))]
        + [dma((2, ny))] * 4
        + [dma((ny, 2)), dma((2, ny))]
        + [dma((ny,)), dma((ny,)), dma((3,)), dma((3,)), dma((3,)), dma((3,))],
        compiler_params=pltpu.CompilerParams(
            collective_id=0, has_side_effects=True, vmem_limit_bytes=60 * 2**20
        ),
    )(gradient, left_basis, right_basis, first_moment, second_moment, weight)


def solution(mesh):
    spec = P("row", "col")
    return jax.shard_map(
        functools.partial(on_device, mesh.shape["row"], mesh.shape["col"]),
        mesh=mesh,
        in_specs=(spec, P("col", "row"), spec, spec, spec, spec),
        out_specs=(spec,) * 4,
        check_vma=False,
    )
```

time: 632 us -> 106 us (0.17)
  waiting for transfers between devices: 605 us -> 0 us
  Pallas kernels: 0 us -> 101 us
  between operations: 14.2 us -> 0.65 us
  matrix products: 9.04 us -> 0 us
    all_gather x4 -> x0, waiting for transfers between devices: 384 us -> none  [the longest x1 135 us: on_device(): lax.all_gather(left_basis, 'col', axis=0, tiled=True)]
    unnamed x7 -> x0, waiting for transfers between devices: 137 us -> none
    pallas_call x0 -> x1, Pallas kernels: none -> 101 us  [on_device(): pl.pallas_call(functools.partial(kernel, ny, nz, tr, tc), out_shape=[f32_...]
    reduce_scatter x1 -> x0, waiting for transfers between devices: 83.9 us -> none  [on_device(): lax.psum_scatter(terms.astype(jnp.bfloat16), 'row', scatter_dimension=0,...]
    dot_general x4 -> x0, matrix products: 9.04 us -> none  [the longest x1 3.24 us: contract_first(): lax.dot_general(left, right, (((0,), (0,)), ((), ())), preferred_element_...]
  transfers between devices with their start and end apart: 6 -> 0, of which waited for: 6 -> 0; matrix products, arithmetic and copies ran while one was open for 1% -> 0% of each run, Pallas kernels for 0% -> 0%
where the time goes in v2:
time: 106 us
  Pallas kernels  101 us (95%)
  local copies, waits for them, and re-layouts  4.14 us (4%)
    pallas_call x1, Pallas kernels, on_device(): pl.pallas_call(functools.partial(kernel, ny, nz, tr, tc), out_shape=[f32_...  101 us
    unnamed x10, local copies, waits for them, and re-layouts  4.14 us

profile of v2, /device:TPU:24, one launch (start us, length us, event | category | flops | bytes accessed | tf_op | source)
XLA Modules:
  0.0 105.5 jit_solution(8340913131723015179)
XLA Ops:
  0.6 100.7 %shard_map.93 = (f32[256,128]{1,0:T(8,128)}, bf16[256,128]{1,0:T(8,128)(2,1)}, f32[256,128]{1,0:T(8,128)}, f32[256,128]{1,0:T(8,128)}) custom-call(bf16[256,128]{1,0:T(8,128)(2,1)} %g_hbm.1, bf16[128,256]{1,0:T(8,128)(2,1)} %l_hbm.1, bf16[256,128]{1,0:T(8,128)(2,1)} %r_hbm.1, f32[256,128]{1,0:T(8,128)} %m1_hbm.1, f32[256,128]{1,0:T(8,128)} %m2_hbm.1, ...), custom_call_target="tpu_custom_call" | custom-call | tf_op jit(solution)/shard_map/pallas_call | solution.py:476
  101.4 0.0 copy-start.2
  101.4 1.6 %copy.14 = f32[256,128]{1,0:T(8,128)} copy(f32[256,128]{1,0:T(8,128)} %get-tuple-element.8) | data formatting | bytes 262144
  103.0 0.0 copy-done.2
  103.0 0.0 copy-start.1
  103.0 0.6 copy.15
  103.6 0.3 copy-done.1
  103.9 0.0 copy-start
  103.9 0.7 copy.16
  104.6 0.3 copy-done
  104.9 0.7 copy.17
Async XLA Ops:
  101.4 1.6 %copy-start.2 = (bf16[256,128]{1,0:T(8,128)(2,1)S(1)}, bf16[256,128]{1,0:T(8,128)(2,1)}, u32[]{:S(2)}) copy-start(bf16[256,128]{1,0:T(8,128)(2,1)} %get-tuple-element.9) | copy-start | bytes 196612
  103.0 0.9 copy-start.1
  103.9 1.0 copy-start

commit v3 on v2

--- a/solution.py
+++ b/solution.py
@@ -15,7 +15,12 @@
 step_count = 20.0
 
 MESH = pl.DeviceIdType.MESH
-G_HOP, L_HOP, U_HOP = 1, 1, 2
+G_UP, G_DN = (2, 2, 1, 1, 1, 1), (2, 2, 1, 1, 1)
+L_UP, L_DN = (1, 1, 1, 1, 1, 1, 1, 1), (1, 1, 1, 1, 1, 1, 1)
+U_UP, U_DN = (2, 2, 2, 2), (2, 2, 2, 1)
+LAG = 1
+PARTS = 2
+RELAY_AT = 5
 L_PARTS = 2
 
 
@@ -39,8 +44,11 @@
     )
 
 
-def hops(distance, hop):
-    return [hop] * (distance // hop) + ([distance % hop] if distance % hop else [])
+def hops(distance, wanted):
+    out = []
+    for hop in wanted:
+        out.append(min(hop, distance - sum(out)))
+    return [hop for hop in out if hop > 0]
 
 
 class Gather:
@@ -90,7 +98,7 @@
 
     def piece(self, k, off, ch):
         i = self.stops[k] + off - 1
-        to = self.at(lax.rem(self.z + self.sign * off + self.nz, self.nz), k == 0 and ch == 1)
+        to = self.at(lax.rem(self.z + self.sign * off + self.nz, self.nz), k == 0 and ch % 2 == 1)
         return copy(self.out.at[ch, i], self.into.at[ch, i], self.send.at[ch, i], self.recv.at[ch, i], to)
 
     def arrived(self, k, ch, total):
@@ -117,15 +125,15 @@
     def sent(self):
         for k, hop in enumerate(self.hops):
             for off in range(1, hop + 1):
-                for ch in range(2):
+                for ch in range(2 * PARTS):
                     self.piece(k, off, ch).wait_send()
 
 
 def kernel(
     ny, nz, tr, tc,
-    g_hbm, l_hbm, r_hbm, m1_hbm, m2_hbm, w_hbm,
-    nw_hbm, up_hbm, nf_hbm, ns_hbm,
-    g_ref, m1_ref, m2_ref, w_ref, nw_ref, up_ref, nf_ref, ns_ref,
+    g_hbm, l_hbm, r_hbm, m1_hbm, m2_hbm,
+    full_hbm, rot_hbm,
+    g_ref, m1_ref, m2_ref, full_ref, rot_ref,
     gbuf, lbuf, lsib, rbuf, ptile, pbuf, xsend, xrecv, nbuf, qsend, qrecv,
     uo_up, ui_up, uo_dn, ui_dn, uo_x, ui_x,
     in_sem, out_sem,
@@ -135,6 +143,7 @@
 ):
     bf16 = jnp.bfloat16
     ratio, hr = tr // tc, tr // 2
+    hp = hr // PARTS
     far_up, far_dn = nz // 2, nz - 1 - nz // 2
     row, col = lax.axis_index("row"), lax.axis_index("col")
     x_hi, y, c = lax.div(row, 2 * ny), lax.rem(lax.div(row, 2), ny), lax.rem(row, 2)
@@ -143,8 +152,8 @@
     diagonal = x_hi == x_lo
 
     own_r = rbuf.at[x_hi, x_lo, y * 2 + c]
-    sources = (g_hbm, l_hbm, r_hbm, m1_hbm, m2_hbm, w_hbm)
-    places = (g_ref, lbuf.at[z], own_r, m1_ref, m2_ref, w_ref)
+    sources = (g_hbm, l_hbm, r_hbm, m1_hbm, m2_hbm)
+    places = (g_ref, lbuf.at[z], own_r, m1_ref, m2_ref)
     loads = [pltpu.make_async_copy(s, d, in_sem.at[i]) for i, (s, d) in enumerate(zip(sources, places))]
     for load in loads:
         load.start()
@@ -199,12 +208,12 @@
         return l_part(z, ch), l_part(z, ch), False
 
     g_rings = [
-        Gather(z, nz, 1, G_HOP, far_up, 2, g_part, g_first, g_us, g_ur, along),
-        Gather(z, nz, -1, G_HOP, far_dn, 2, g_part, g_first, g_ds, g_dr, along),
+        Gather(z, nz, 1, G_UP, far_up, 2, g_part, g_first, g_us, g_ur, along),
+        Gather(z, nz, -1, G_DN, far_dn, 2, g_part, g_first, g_ds, g_dr, along),
     ]
     l_rings = [
-        Gather(z, nz, 1, L_HOP, far_up, L_PARTS, l_part, l_first, l_us, l_ur, along),
-        Gather(z, nz, -1, L_HOP, far_dn, L_PARTS, l_part, l_first, l_ds, l_dr, along),
+        Gather(z, nz, 1, L_UP, far_up, L_PARTS, l_part, l_first, l_us, l_ur, along),
+        Gather(z, nz, -1, L_DN, far_dn, L_PARTS, l_part, l_first, l_ds, l_dr, along),
     ]
 
     pending = [ring.sent for ring in g_rings + l_rings]
@@ -242,25 +251,26 @@
     ring_step(g_rings, 0)
     g_beside().start()
     loads[1].wait()
-    ring_step(l_rings, 0)
     loads[2].wait()
     loop(4 * ny - 1, lambda i: r_out(i + 1).start())
     r_relay(0, True)[1].start()
-
     pending.append(g_beside().wait_send)
     pending.append(lambda: loop(4 * ny - 1, lambda i: r_out(i + 1).wait_send()))
     pending.append(lambda: loop(4 * ny, lambda i: r_relay(i, True)[1].wait_send()))
+
     g_steps, l_steps = len(g_rings[0].hops), len(l_rings[0].hops)
-    relayed, rounds = 1, max(g_steps, l_steps)
-    for k in range(1, rounds):
-        ring_step(g_rings, k)
-        ring_step(l_rings, k)
-        if k >= rounds // 2:
-            left = rounds - k
+    relayed, l_done = 1, 0
+    for k in range(g_steps):
+        if k > 0:
+            ring_step(g_rings, k)
+        if k >= LAG and l_done < l_steps:
+            ring_step(l_rings, l_done)
+            l_done += 1
+        if k >= min(RELAY_AT, g_steps - 1):
+            left = g_steps - k
             upto = relayed + (4 * ny - relayed + left - 1) // left
             lax.fori_loop(relayed, upto, lambda i, carry: (r_pass(i), carry)[1], 0)
             relayed = upto
-    lax.fori_loop(relayed, 4 * ny, lambda i, carry: (r_pass(i), carry)[1], 0)
     loop(4 * ny, lambda i: r_relay(i, False)[1].wait_recv())
     for ring in g_rings:
         ring.finish()
@@ -298,6 +308,8 @@
     def _():
         pbuf[y * 2 + c, x_lo] = ptile[...]
 
+    for k in range(l_done, l_steps):
+        ring_step(l_rings, k)
     for ring in l_rings:
         ring.finish()
 
@@ -359,29 +371,32 @@
     origins = ((c, 1 - x_lo), (sib, 1 - x_lo), (sib, x_lo))
     for k in range(3):
         share_n(k, targets[k], c, x_lo).start()
-    nf_ref[...] = new_first
-    ns_ref[...] = new_second
+    rot_ref[...] = rotated
     saves = [
-        pltpu.make_async_copy(s, d, out_sem.at[i])
-        for i, (s, d) in enumerate(
-            ((nf_ref, nf_hbm), (ns_ref, ns_hbm), (nw_ref, nw_hbm), (up_ref, up_hbm))
-        )
+        pltpu.make_async_copy(rot_ref, rot_hbm, out_sem.at[0]),
+        pltpu.make_async_copy(full_ref, full_hbm, out_sem.at[1]),
     ]
     saves[0].start()
-    saves[1].start()
-    pending += [saves[0].wait, saves[1].wait]
+    pending.append(saves[0].wait)
     loop(ny, lambda yy: share_l(yy).wait_recv())
     for k in range(3):
         share_n(k, targets[k], *origins[k]).wait_recv()
         pending.append(share_n(k, targets[k], c, x_lo).wait_send)
 
-    def q_out(dy, half):
+    def q_out(dy, half, part):
         yy = lax.rem(y + dy, ny)
         is_self = diagonal & (half == x_lo) & (dy == 0)
-        to = device(x_lo, yy, c, half, z)
         return is_self, copy(
-            qsend.at[dy, half], qrecv.at[x_hi, y], q_s.at[dy, half], q_r.at[x_hi, y], to
+            qsend.at[dy, half, part],
+            qrecv.at[x_hi, y, part],
+            q_s.at[dy, half, part],
+            q_r.at[x_hi, y, part],
+            device(x_lo, yy, c, half, z),
         )
+
+    def q_start(dy, half, part):
+        is_self, send = q_out(dy, half, part)
+        pl.when(~is_self)(send.start)
 
     own_n = jnp.concatenate([nbuf[c, 0], nbuf[c, 1]], axis=1)
     sib_n = jnp.concatenate([nbuf[sib, 0], nbuf[sib, 1]], axis=1)
@@ -392,68 +407,84 @@
         sib_l = lsib[yy].reshape(tr, tr)
         block = (dot(own_l, own_n, 1, 0) + dot(sib_l, sib_n, 1, 0)).astype(bf16)
         for half in range(2):
-            qsend[dy, half] = block[half * hr : (half + 1) * hr]
-            is_self, send = q_out(dy, half)
-            pl.when(~is_self)(send.start)
+            for part in range(PARTS):
+                at = half * hr + part * hp
+                qsend[dy, half, part] = block[at : at + hp]
+            q_start(dy, half, 0)
+    for part in range(1, PARTS):
+        for step in range(ny):
+            for half in range(2):
+                q_start((step + 1) % ny, half, part)
 
     @pl.when(diagonal)
     def _():
         qrecv[x_hi, y] = qsend[0, x_lo]
 
-    total = jnp.zeros((hr, 2 * tc), jnp.float32)
-    for dy in range(ny):
-        yy = lax.rem(y + dy, ny)
-        for hi in range(2):
-            is_self = diagonal & (hi == x_hi) & (dy == 0)
-            arrive = copy(ptile, qrecv.at[hi, yy], q_s.at[0, 0], q_r.at[hi, yy], beside)
-            pl.when(~is_self)(arrive.wait_recv)
-            total += qrecv[hi, yy].astype(jnp.float32)
-    q = total.astype(bf16)
+    def q_sum(part):
+        total = jnp.zeros((hp, 2 * tc), jnp.float32)
+        for dy in range(ny):
+            yy = lax.rem(y + dy, ny)
+            for hi in range(2):
+                is_self = diagonal & (hi == x_hi) & (dy == 0)
+                slot = qrecv.at[hi, yy, part]
+                arrive = copy(slot, slot, q_s.at[0, 0, part], q_r.at[hi, yy, part], beside)
+                pl.when(~is_self)(arrive.wait_recv)
+                total += qrecv[hi, yy, part].astype(jnp.float32)
+        return total.astype(bf16)
 
     def q_sent(i):
-        is_self, send = q_out(lax.rem(i, ny), lax.div(i, ny))
-        pl.when(~is_self)(send.wait_send)
+        for part in range(PARTS):
+            is_self, send = q_out(lax.rem(i, ny), lax.div(i, ny), part)
+            pl.when(~is_self)(send.wait_send)
 
     pending.append(lambda: loop(2 * ny, q_sent))
+
+    q = [None] * PARTS
 
     def u_own(away, ch):
         d = lax.rem(z + away + nz, nz)
-        hi = x_lo if ch == 0 else 1 - x_lo
+        hi = x_lo if ch % 2 == 0 else 1 - x_lo
         rows = pl.ds(pl.multiple_of(lax.rem(d, ratio) * tc, tc), tc)
         at = lax.div(d, ratio)
         right = jnp.concatenate([rbuf[hi, 0, at, rows], rbuf[hi, 1, at, rows]], axis=1)
-        return dot(q, right, 1, 1)
+        return dot(q[ch // 2], right, 1, 1)
 
     u_rings = [
-        Scatter(z, nz, 1, U_HOP, far_up, u_own, uo_up, ui_up, u_us, u_ur, along),
-        Scatter(z, nz, -1, U_HOP, far_dn, u_own, uo_dn, ui_dn, u_ds, u_dr, along),
+        Scatter(z, nz, 1, U_UP, far_up, u_own, uo_up, ui_up, u_us, u_ur, along),
+        Scatter(z, nz, -1, U_DN, far_dn, u_own, uo_dn, ui_dn, u_ds, u_dr, along),
     ]
-    u_beside = copy(uo_x, ui_x, x_s.at[2], x_r.at[2], beside)
-    for k in reversed(range(len(u_rings[0].hops))):
-        for ch in (1, 0):
+
+    def u_beside(part):
+        return copy(uo_x.at[part], ui_x.at[part], x_s.at[2 + part], x_r.at[2 + part], beside)
+
+    first_step = len(u_rings[0].hops) - 1
+    for k in range(first_step, -1, -1):
+        for part in range(PARTS):
+            if k == first_step:
+                q[part] = q_sum(part)
+            for ch in (2 * part + 1, 2 * part):
+                for ring in u_rings:
+                    ring.far(k, ch)
+                for ring in u_rings:
+                    ring.near(k, ch)
+            if k == first_step:
+                uo_x[part] = u_own(0, 2 * part + 1).astype(bf16)
+                u_beside(part).start()
+
+    for part in range(PARTS):
+        own = u_own(0, 2 * part)
+        u_beside(part).wait_recv()
+        for which, total, ch in (
+            (1 - x_lo, ui_x[part].astype(jnp.float32), 2 * part + 1),
+            (x_lo, own, 2 * part),
+        ):
             for ring in u_rings:
-                ring.far(k, ch)
-            for ring in u_rings:
-                ring.near(k, ch)
-        if k == len(u_rings[0].hops) - 1:
-            uo_x[...] = u_own(0, 1).astype(bf16)
-            u_beside.start()
-
-    def finish(which, total, ch):
-        for ring in u_rings:
-            total = ring.arrived(0, ch, total)
-        rows = pl.ds(pl.multiple_of(which * hr, hr), hr)
-        weight = w_ref[rows, :]
-        up_ref[rows, :] = total.astype(bf16)
-        nw_ref[rows, :] = weight - learn_rate * (total + weight_decay * weight)
-
-    mine = u_own(0, 0)
-    u_beside.wait_recv()
-    finish(1 - x_lo, ui_x[...].astype(jnp.float32), 1)
-    finish(x_lo, mine, 0)
-    saves[2].start()
-    saves[3].start()
-    pending += [saves[2].wait, saves[3].wait, u_beside.wait_send]
+                total = ring.arrived(0, ch, total)
+            rows = pl.ds(pl.multiple_of(which * hr + part * hp, hp), hp)
+            full_ref[rows, :] = total
+        pending.append(u_beside(part).wait_send)
+    saves[1].start()
+    pending.append(saves[1].wait)
     pending += [ring.sent for ring in u_rings]
 
     for wait in pending:
@@ -466,6 +497,7 @@
     up, dn = nz // 2, nz - 1 - nz // 2
     bf16, f32 = jnp.bfloat16, jnp.float32
     ratio, hr = tr // tc, tr // 2
+    hp = hr // PARTS
     dma = pltpu.SemaphoreType.DMA
     f32_tile = jax.ShapeDtypeStruct((tr, tc), f32)
     anywhere = pl.BlockSpec(memory_space=pl.ANY)
@@ -473,18 +505,15 @@
     def ring(pieces):
         return [dma((pieces, up)), dma((pieces, up)), dma((pieces, dn)), dma((pieces, dn))]
 
-    return pl.pallas_call(
+    full_update, rotated = pl.pallas_call(
         functools.partial(kernel, ny, nz, tr, tc),
-        out_shape=[f32_tile, jax.ShapeDtypeStruct((tr, tc), bf16), f32_tile, f32_tile],
-        in_specs=[anywhere] * 6,
-        out_specs=[anywhere] * 4,
+        out_shape=[f32_tile, f32_tile],
+        in_specs=[anywhere] * 5,
+        out_specs=[anywhere] * 2,
         scratch_shapes=[
             pltpu.VMEM((tr, tc), bf16),
             pltpu.VMEM((tr, tc), f32),
             pltpu.VMEM((tr, tc), f32),
-            pltpu.VMEM((tr, tc), f32),
-            pltpu.VMEM((tr, tc), f32),
-            pltpu.VMEM((tr, tc), bf16),
             pltpu.VMEM((tr, tc), f32),
             pltpu.VMEM((tr, tc), f32),
             pltpu.VMEM((2, nz, hr, tc), bf16),
@@ -496,28 +525,33 @@
             pltpu.VMEM((tr, tc), bf16),
             pltpu.VMEM((tr, tc), bf16),
             pltpu.VMEM((2, 2, tr, tc), bf16),
-            pltpu.VMEM((ny, 2, hr, 2 * tc), bf16),
-            pltpu.VMEM((2, ny, hr, 2 * tc), bf16),
-            pltpu.VMEM((2, up, hr, tc), bf16),
-            pltpu.VMEM((2, up, hr, tc), bf16),
-            pltpu.VMEM((2, dn, hr, tc), bf16),
-            pltpu.VMEM((2, dn, hr, tc), bf16),
-            pltpu.VMEM((hr, tc), bf16),
-            pltpu.VMEM((hr, tc), bf16),
-            dma((6,)),
-            dma((4,)),
+            pltpu.VMEM((ny, 2, PARTS, hp, 2 * tc), bf16),
+            pltpu.VMEM((2, ny, PARTS, hp, 2 * tc), bf16),
+            pltpu.VMEM((2 * PARTS, up, hp, tc), bf16),
+            pltpu.VMEM((2 * PARTS, up, hp, tc), bf16),
+            pltpu.VMEM((2 * PARTS, dn, hp, tc), bf16),
+            pltpu.VMEM((2 * PARTS, dn, hp, tc), bf16),
+            pltpu.VMEM((PARTS, hp, tc), bf16),
+            pltpu.VMEM((PARTS, hp, tc), bf16),
+            dma((5,)),
+            dma((2,)),
         ]
         + ring(2)
         + ring(L_PARTS)
-        + ring(2)
+        + ring(2 * PARTS)
         + [dma((4 * ny,)), dma((4, ny)), dma((4, ny)), dma((4, ny))]
         + [dma((2, ny))] * 4
-        + [dma((ny, 2)), dma((2, ny))]
-        + [dma((ny,)), dma((ny,)), dma((3,)), dma((3,)), dma((3,)), dma((3,))],
+        + [dma((ny, 2, PARTS)), dma((2, ny, PARTS))]
+        + [dma((ny,)), dma((ny,)), dma((2 + PARTS,)), dma((2 + PARTS,)), dma((3,)), dma((3,))],
         compiler_params=pltpu.CompilerParams(
             collective_id=0, has_side_effects=True, vmem_limit_bytes=60 * 2**20
         ),
-    )(gradient, left_basis, right_basis, first_moment, second_moment, weight)
+    )(gradient, left_basis, right_basis, first_moment, second_moment)
+    new_first = beta_one * first_moment + (1.0 - beta_one) * rotated
+    new_second = beta_two * second_moment + (1.0 - beta_two) * rotated * rotated
+    update = full_update.astype(bf16)
+    new_weight = weight - learn_rate * (full_update + weight_decay * weight)
+    return new_weight, update, new_first, new_second
 
 
 def solution(mesh):

time: 106 us -> 97.4 us (0.919)
  Pallas kernels: 101 us -> 94.4 us
  local copies, waits for them, and re-layouts: 4.14 us -> 0.01 us
  other arithmetic: 0 us -> 1.82 us
    pallas_call x1, Pallas kernels: 101 us -> 94.4 us  [on_device(): pl.pallas_call(functools.partial(kernel, ny, nz, tr, tc), out_shape=[f32_...]
    unnamed x10 -> x6, local copies, waits for them, and re-layouts: 4.14 us -> 0.01 us
    add x0 -> x1, other arithmetic: none -> 1.82 us  [on_device(): new_second = beta_two * second_moment + (1.0 - beta_two) * rotated * rotated]
where the time goes in v3:
time: 97.4 us; the launch traced here: 96.9 us
  Pallas kernels  94.4 us (97%)
  other arithmetic  1.82 us (2%)
    pallas_call x1, Pallas kernels, on_device(): pl.pallas_call(functools.partial(kernel, ny, nz, tr, tc), out_shape=[f32_...  94.4 us

profile of v3, /device:TPU:24, one launch (start us, length us, event | category | flops | bytes accessed | tf_op | source)
XLA Modules:
  0.0 96.9 jit_solution(229119066579508827)
XLA Ops:
  0.6 0.0 copy-start.1
  0.6 0.0 copy-start
  0.7 0.0 copy-start.2
  0.7 94.4 %shard_map.93 = (f32[256,128]{1,0:T(8,128)}, f32[256,128]{1,0:T(8,128)}) custom-call(bf16[256,128]{1,0:T(8,128)(2,1)} %g_hbm.1, bf16[128,256]{1,0:T(8,128)(2,1)} %l_hbm.1, bf16[256,128]{1,0:T(8,128)(2,1)} %r_hbm.1, f32[256,128]{1,0:T(8,128)} %m1_hbm.1, f32[256,128]{1,0:T(8,128)} %m2_hbm.1), custom_call_target="tpu_custom_call" | custom-call | tf_op jit(solution)/shard_map/pallas_call | solution.py:508
  95.0 0.0 copy-done.1
  95.1 0.0 copy-done
  95.1 0.0 copy-done.2
  95.1 1.8 %fusion = (f32[256,128]{1,0:T(8,128)}, f32[256,128]{1,0:T(8,128)}, f32[256,128]{1,0:T(8,128)}, bf16[256,128]{1,0:T(8,128)(2,1)}) fusion(f32[256,128]{1,0:T(8,128)} %get-tuple-element.7, f32[256,128]{1,0:T(8,128)S(1)} %copy-done.1, f32[256,128]{1,0:T(8,128)S(1)} %copy-done, f32[256,128]{1,0:T(8,128)S(1)} %copy-done.2, f32[256,128]{1,0:T(8,128)} %get-tuple-element.6), kind=kLoop, calls=%fused_computation.1 | loop fusion | flops 393216 | bytes 1114112 | tf_op jit(solution)/shard_map/add | solution.py:551
Async XLA Ops:
  0.6 94.4 %copy-start.1 = (f32[256,128]{1,0:T(8,128)S(1)}, f32[256,128]{1,0:T(8,128)}, u32[]{:S(2)}) copy-start(f32[256,128]{1,0:T(8,128)} %m2_hbm.1) | copy-start | bytes 393220
  0.6 94.4 %copy-start = (f32[256,128]{1,0:T(8,128)S(1)}, f32[256,128]{1,0:T(8,128)}, u32[]{:S(2)}) copy-start(f32[256,128]{1,0:T(8,128)} %m1_hbm.1) | copy-start | bytes 393220
  0.7 94.4 %copy-start.2 = (f32[256,128]{1,0:T(8,128)S(1)}, f32[256,128]{1,0:T(8,128)}, u32[]{:S(2)}) copy-start(f32[256,128]{1,0:T(8,128)} %param.11) | copy-start | bytes 393220

commit v4 on v3

--- a/solution.py
+++ b/solution.py
@@ -15,11 +15,12 @@
 step_count = 20.0
 
 MESH = pl.DeviceIdType.MESH
-G_UP, G_DN = (2, 2, 1, 1, 1, 1), (2, 2, 1, 1, 1)
+G_UP, G_DN = (2, 2, 2, 1, 1), (2, 2, 2, 1)
 L_UP, L_DN = (1, 1, 1, 1, 1, 1, 1, 1), (1, 1, 1, 1, 1, 1, 1)
 U_UP, U_DN = (2, 2, 2, 2), (2, 2, 2, 1)
 LAG = 1
 PARTS = 2
+G_PARTS = 1
 RELAY_AT = 5
 L_PARTS = 2
 
@@ -53,7 +54,7 @@
 
 class Gather:
     def __init__(self, z, nz, sign, hop, distance, pieces, part, first, send, recv, at):
-        self.z, self.nz, self.sign, self.pieces = z, nz, sign, pieces
+        self.z, self.nz, self.sign, self.pieces = z, nz, sign, tuple(pieces)
         self.part, self.first, self.send, self.recv, self.at = part, first, send, recv, at
         self.hops = hops(distance, hop)
         self.stops = [sum(self.hops[:k]) for k in range(len(self.hops) + 1)]
@@ -75,23 +76,24 @@
             for off in range(self.hops[k], 0, -1):
                 self.piece(k, off, ch, True).start()
 
-    def finish(self):
+    def finish(self, pieces):
         last = len(self.hops) - 1
         for k, hop in enumerate(self.hops):
             for off in range(1, hop + (k == last)):
-                for ch in range(self.pieces):
-                    self.piece(k, off, ch, False).wait_recv()
+                for ch in self.pieces:
+                    if ch in pieces:
+                        self.piece(k, off, ch, False).wait_recv()
 
     def sent(self):
         for k, hop in enumerate(self.hops):
             for off in range(1, hop + 1):
-                for ch in range(self.pieces):
+                for ch in self.pieces:
                     self.piece(k, off, ch, True).wait_send()
 
 
 class Scatter:
-    def __init__(self, z, nz, sign, hop, distance, own, out, into, send, recv, at):
-        self.z, self.nz, self.sign = z, nz, sign
+    def __init__(self, z, nz, sign, hop, distance, pieces, own, out, into, send, recv, at):
+        self.z, self.nz, self.sign, self.pieces = z, nz, sign, tuple(pieces)
         self.own, self.out, self.into, self.send, self.recv, self.at = own, out, into, send, recv, at
         self.hops = hops(distance, hop)
         self.stops = [sum(self.hops[:k]) for k in range(len(self.hops) + 1)]
@@ -102,21 +104,21 @@
         return copy(self.out.at[ch, i], self.into.at[ch, i], self.send.at[ch, i], self.recv.at[ch, i], to)
 
     def arrived(self, k, ch, total):
-        if k < len(self.hops):
+        if k < len(self.hops) and ch in self.pieces:
             for off in range(1, self.hops[k] + 1):
                 self.piece(k, off, ch).wait_recv()
                 total += self.into[ch, self.stops[k] + off - 1].astype(jnp.float32)
         return total
 
     def far(self, k, ch):
-        if k < len(self.hops):
+        if k < len(self.hops) and ch in self.pieces:
             stop = self.stops[k + 1]
             total = self.arrived(k + 1, ch, self.own(self.sign * stop, ch))
             self.out[ch, stop - 1] = total.astype(jnp.bfloat16)
             self.piece(k, self.hops[k], ch).start()
 
     def near(self, k, ch):
-        if k < len(self.hops):
+        if k < len(self.hops) and ch in self.pieces:
             for off in range(1, self.hops[k]):
                 stop = self.stops[k] + off
                 self.out[ch, stop - 1] = self.own(self.sign * stop, ch).astype(jnp.bfloat16)
@@ -125,7 +127,7 @@
     def sent(self):
         for k, hop in enumerate(self.hops):
             for off in range(1, hop + 1):
-                for ch in range(2 * PARTS):
+                for ch in self.pieces:
                     self.piece(k, off, ch).wait_send()
 
 
@@ -190,14 +192,17 @@
     loop(4 * ny - 1, greet_plane)
     pl.semaphore_wait(barrier, 2 * len(near) + 2 + 4 * ny - 1)
 
+    hg = hr // G_PARTS
+
     def g_part(tile, ch):
-        return gbuf.at[x_lo if ch == 0 else 1 - x_lo, tile]
-
-    def g_half(which):
-        return g_ref.at[pl.ds(pl.multiple_of(which * hr, hr), hr)]
+        return gbuf.at[ch // 2, x_lo if ch % 2 == 0 else 1 - x_lo, tile]
+
+    def g_rows(which, part):
+        return g_ref.at[pl.ds(pl.multiple_of(which * hr + part * hg, hg), hg)]
 
     def g_first(ch):
-        return g_half(x_lo if ch == 0 else 1 - x_lo), gbuf.at[x_lo, z], ch == 1
+        which = x_lo if ch % 2 == 0 else 1 - x_lo
+        return g_rows(which, ch // 2), gbuf.at[ch // 2, x_lo, z], ch % 2 == 1
 
     lrows = tc // L_PARTS
 
@@ -207,24 +212,32 @@
     def l_first(ch):
         return l_part(z, ch), l_part(z, ch), False
 
+    own_g, other_g = range(0, 2 * G_PARTS, 2), range(1, 2 * G_PARTS, 2)
     g_rings = [
-        Gather(z, nz, 1, G_UP, far_up, 2, g_part, g_first, g_us, g_ur, along),
-        Gather(z, nz, -1, G_DN, far_dn, 2, g_part, g_first, g_ds, g_dr, along),
+        Gather(z, nz, 1, G_UP, far_up, own_g, g_part, g_first, g_us, g_ur, along),
+        Gather(z, nz, -1, G_DN, far_dn, own_g, g_part, g_first, g_ds, g_dr, along),
+        Gather(z, nz, -1, G_UP, far_up, other_g, g_part, g_first, g_ds, g_dr, along),
+        Gather(z, nz, 1, G_DN, far_dn, other_g, g_part, g_first, g_us, g_ur, along),
     ]
+    l_all = range(L_PARTS)
     l_rings = [
-        Gather(z, nz, 1, L_UP, far_up, L_PARTS, l_part, l_first, l_us, l_ur, along),
-        Gather(z, nz, -1, L_DN, far_dn, L_PARTS, l_part, l_first, l_ds, l_dr, along),
+        Gather(z, nz, 1, L_UP, far_up, l_all, l_part, l_first, l_us, l_ur, along),
+        Gather(z, nz, -1, L_DN, far_dn, l_all, l_part, l_first, l_ds, l_dr, along),
     ]
 
     pending = [ring.sent for ring in g_rings + l_rings]
 
     def ring_step(rings, k):
-        for ch in range(rings[0].pieces):
+        for ch in sorted({ch for ring in rings for ch in ring.pieces}):
             for ring in rings:
-                ring.step(k, ch)
-
-    def g_beside():
-        return copy(g_half(1 - x_lo), gbuf.at[x_lo, z], x_s.at[0], x_r.at[0], beside)
+                if ch in ring.pieces:
+                    ring.step(k, ch)
+
+    def g_beside(part):
+        sem = 2 + PARTS + part
+        return copy(
+            g_rows(1 - x_lo, part), gbuf.at[part, x_lo, z], x_s.at[sem], x_r.at[sem], beside
+        )
 
     def r_out(i):
         hi, lo, yy = in_plane(i)
@@ -246,15 +259,17 @@
         send.start()
 
     loads[0].wait()
-    g_ref_ready = pl.ds(pl.multiple_of(x_lo * hr, hr), hr)
-    gbuf[x_lo, z] = g_ref[g_ref_ready, :]
+    for part in range(G_PARTS):
+        at = pl.ds(pl.multiple_of(x_lo * hr + part * hg, hg), hg)
+        gbuf[part, x_lo, z] = g_ref[at, :]
     ring_step(g_rings, 0)
-    g_beside().start()
+    for part in range(G_PARTS):
+        g_beside(part).start()
+        pending.append(g_beside(part).wait_send)
     loads[1].wait()
     loads[2].wait()
     loop(4 * ny - 1, lambda i: r_out(i + 1).start())
     r_relay(0, True)[1].start()
-    pending.append(g_beside().wait_send)
     pending.append(lambda: loop(4 * ny - 1, lambda i: r_out(i + 1).wait_send()))
     pending.append(lambda: loop(4 * ny, lambda i: r_relay(i, True)[1].wait_send()))
 
@@ -272,35 +287,38 @@
             lax.fori_loop(relayed, upto, lambda i, carry: (r_pass(i), carry)[1], 0)
             relayed = upto
     loop(4 * ny, lambda i: r_relay(i, False)[1].wait_recv())
-    for ring in g_rings:
-        ring.finish()
-    g_beside().wait_recv()
-
-    partial = jnp.zeros((hr, 2 * tc), jnp.float32)
-    for hi in range(2):
-        for b in range(2 * ny):
-            left = jnp.concatenate([gbuf[hi, b * ratio + k] for k in range(ratio)], axis=1)
-            right = jnp.concatenate([rbuf[hi, 0, b], rbuf[hi, 1, b]], axis=1)
-            partial += dot(left, right, 1, 0)
-    ptile[...] = partial.astype(bf16)
-
-    own_p = pbuf.at[y * 2 + c, x_lo]
-
-    def p_out(i):
-        hi, dy = lax.div(i, ny), lax.rem(i, ny)
+
+    def p_out(i, part):
+        hi, dy = lax.rem(1 - x_hi + lax.div(i, ny), 2), lax.rem(i + 2, ny)
         is_self = diagonal & (hi == x_hi) & (dy == 0)
         to = device(hi, lax.rem(y + dy, ny), c, x_hi, z)
-        return is_self, copy(ptile, own_p, p_s.at[hi, dy], p_r.at[x_lo, y], to)
-
-    def p_start(i):
-        is_self, send = p_out(i)
-        pl.when(~is_self)(send.start)
-
-    loop(2 * ny, p_start)
+        slot = pbuf.at[y * 2 + c, x_lo, part]
+        return is_self, copy(ptile.at[part], slot, p_s.at[hi, dy, part], p_r.at[x_lo, y, part], to)
+
+    for part in range(G_PARTS):
+        for ring in g_rings:
+            ring.finish((2 * part, 2 * part + 1))
+        g_beside(part).wait_recv()
+        partial = jnp.zeros((hg, 2 * tc), jnp.float32)
+        for hi in range(2):
+            for b in range(2 * ny):
+                left = jnp.concatenate(
+                    [gbuf[part, hi, b * ratio + k] for k in range(ratio)], axis=1
+                )
+                right = jnp.concatenate([rbuf[hi, 0, b], rbuf[hi, 1, b]], axis=1)
+                partial += dot(left, right, 1, 0)
+        ptile[part] = partial.astype(bf16)
+
+        def p_start(i):
+            is_self, send = p_out(i, part)
+            pl.when(~is_self)(send.start)
+
+        loop(2 * ny, p_start)
 
     def p_sent(i):
-        is_self, send = p_out(i)
-        pl.when(~is_self)(send.wait_send)
+        for part in range(G_PARTS):
+            is_self, send = p_out(i, part)
+            pl.when(~is_self)(send.wait_send)
 
     pending.append(lambda: loop(2 * ny, p_sent))
 
@@ -311,18 +329,19 @@
     for k in range(l_done, l_steps):
         ring_step(l_rings, k)
     for ring in l_rings:
-        ring.finish()
+        ring.finish(l_all)
 
     def share_l(yy):
         rows = pl.ds((2 * yy + sib) * ratio, ratio)
         return copy(lbuf.at[rows], lsib.at[yy], lsib_s.at[yy], lsib_r.at[yy], sibling)
 
-    def p_relay(dy, lo, own):
+    def p_relay(dy, lo, part, own):
         yy = lax.rem(y + dy, ny)
-        slot = pbuf.at[yy * 2 + (c if own else sib), lo]
+        slot = pbuf.at[yy * 2 + (c if own else sib), lo, part]
         is_self = diagonal & (lo == x_lo) & (dy == 0)
-        arrive = copy(ptile, slot, p_s.at[0, 0], p_r.at[lo, yy], sibling)
-        return is_self, arrive, copy(slot, slot, psib_s.at[lo, yy], psib_r.at[lo, yy], sibling)
+        arrive = copy(slot, slot, p_s.at[0, 0, part], p_r.at[lo, yy, part], sibling)
+        at = (lo, yy, part)
+        return is_self, arrive, copy(slot, slot, psib_s.at[at], psib_r.at[at], sibling)
 
     partial = jnp.zeros((tr, 2 * tc), jnp.float32)
 
@@ -331,20 +350,25 @@
         left = lbuf[pl.ds(block * ratio, ratio)].reshape(tr, tr)
         return partial + dot(left, pbuf[block].reshape(tr, 2 * tc), 0, 0)
 
+    for part in range(G_PARTS):
+        for dy in range(ny):
+            for lo in range(2):
+                is_self, arrive, send = p_relay(dy, lo, part, True)
+                pl.when(~is_self)(arrive.wait_recv)
+                send.start()
+            if part == G_PARTS - 1:
+                partial = rotate(partial, dy, c)
     for dy in range(ny):
         for lo in range(2):
-            is_self, arrive, send = p_relay(dy, lo, True)
-            pl.when(~is_self)(arrive.wait_recv)
-            send.start()
-        partial = rotate(partial, dy, c)
-    for dy in range(ny):
-        for lo in range(2):
-            p_relay(dy, lo, False)[2].wait_recv()
+            for part in range(G_PARTS):
+                p_relay(dy, lo, part, False)[2].wait_recv()
         partial = rotate(partial, dy, sib)
 
-    pending.append(
-        lambda: loop(2 * ny, lambda i: p_relay(lax.rem(i, ny), lax.div(i, ny), True)[2].wait_send())
-    )
+    def p_relayed(i):
+        for part in range(G_PARTS):
+            p_relay(lax.rem(i, ny), lax.div(i, ny), part, True)[2].wait_send()
+
+    pending.append(lambda: loop(2 * ny, p_relayed))
     first, second = partial[:, :tc], partial[:, tc:]
     xsend[...] = jnp.where(x_lo == 0, second, first).astype(bf16)
     swap = copy(xsend, xrecv, x_s.at[1], x_r.at[1], beside)
@@ -449,9 +473,12 @@
         right = jnp.concatenate([rbuf[hi, 0, at, rows], rbuf[hi, 1, at, rows]], axis=1)
         return dot(q[ch // 2], right, 1, 1)
 
+    own_u, other_u = range(0, 2 * PARTS, 2), range(1, 2 * PARTS, 2)
     u_rings = [
-        Scatter(z, nz, 1, U_UP, far_up, u_own, uo_up, ui_up, u_us, u_ur, along),
-        Scatter(z, nz, -1, U_DN, far_dn, u_own, uo_dn, ui_dn, u_ds, u_dr, along),
+        Scatter(z, nz, 1, U_UP, far_up, own_u, u_own, uo_up, ui_up, u_us, u_ur, along),
+        Scatter(z, nz, -1, U_DN, far_dn, own_u, u_own, uo_dn, ui_dn, u_ds, u_dr, along),
+        Scatter(z, nz, -1, U_UP, far_up, other_u, u_own, uo_dn, ui_dn, u_ds, u_dr, along),
+        Scatter(z, nz, 1, U_DN, far_dn, other_u, u_own, uo_up, ui_up, u_us, u_ur, along),
     ]
 
     def u_beside(part):
@@ -494,16 +521,16 @@
 def on_device(n_row, n_col, gradient, left_basis, right_basis, first_moment, second_moment, weight):
     ny, nz = n_row // 4, n_col // 2
     tr, tc = gradient.shape
-    up, dn = nz // 2, nz - 1 - nz // 2
+    up = nz // 2
     bf16, f32 = jnp.bfloat16, jnp.float32
     ratio, hr = tr // tc, tr // 2
-    hp = hr // PARTS
+    hp, hg = hr // PARTS, hr // G_PARTS
     dma = pltpu.SemaphoreType.DMA
     f32_tile = jax.ShapeDtypeStruct((tr, tc), f32)
     anywhere = pl.BlockSpec(memory_space=pl.ANY)
 
     def ring(pieces):
-        return [dma((pieces, up)), dma((pieces, up)), dma((pieces, dn)), dma((pieces, dn))]
+        return [dma((pieces, up))] * 4
 
     full_update, rotated = pl.pallas_call(
         functools.partial(kernel, ny, nz, tr, tc),
@@ -516,12 +543,12 @@
             pltpu.VMEM((tr, tc), f32),
             pltpu.VMEM((tr, tc), f32),
             pltpu.VMEM((tr, tc), f32),
-            pltpu.VMEM((2, nz, hr, tc), bf16),
+            pltpu.VMEM((G_PARTS, 2, nz, hg, tc), bf16),
             pltpu.VMEM((nz, tc, tr), bf16),
             pltpu.VMEM((ny, ratio, tc, tr), bf16),
             pltpu.VMEM((2, 2, 2 * ny, tr, tc), bf16),
-            pltpu.VMEM((hr, 2 * tc), bf16),
-            pltpu.VMEM((2 * ny, 2, hr, 2 * tc), bf16),
+            pltpu.VMEM((G_PARTS, hg, 2 * tc), bf16),
+            pltpu.VMEM((2 * ny, 2, G_PARTS, hg, 2 * tc), bf16),
             pltpu.VMEM((tr, tc), bf16),
             pltpu.VMEM((tr, tc), bf16),
             pltpu.VMEM((2, 2, tr, tc), bf16),
@@ -529,20 +556,20 @@
             pltpu.VMEM((2, ny, PARTS, hp, 2 * tc), bf16),
             pltpu.VMEM((2 * PARTS, up, hp, tc), bf16),
             pltpu.VMEM((2 * PARTS, up, hp, tc), bf16),
-            pltpu.VMEM((2 * PARTS, dn, hp, tc), bf16),
-            pltpu.VMEM((2 * PARTS, dn, hp, tc), bf16),
+            pltpu.VMEM((2 * PARTS, up, hp, tc), bf16),
+            pltpu.VMEM((2 * PARTS, up, hp, tc), bf16),
             pltpu.VMEM((PARTS, hp, tc), bf16),
             pltpu.VMEM((PARTS, hp, tc), bf16),
             dma((5,)),
             dma((2,)),
         ]
-        + ring(2)
+        + ring(2 * G_PARTS)
         + ring(L_PARTS)
         + ring(2 * PARTS)
         + [dma((4 * ny,)), dma((4, ny)), dma((4, ny)), dma((4, ny))]
-        + [dma((2, ny))] * 4
+        + [dma((2, ny, G_PARTS))] * 4
         + [dma((ny, 2, PARTS)), dma((2, ny, PARTS))]
-        + [dma((ny,)), dma((ny,)), dma((2 + PARTS,)), dma((2 + PARTS,)), dma((3,)), dma((3,))],
+        + [dma((ny,)), dma((ny,)), dma((2 + PARTS + G_PARTS,)), dma((2 + PARTS + G_PARTS,)), dma((3,)), dma((3,))],
         compiler_params=pltpu.CompilerParams(
             collective_id=0, has_side_effects=True, vmem_limit_bytes=60 * 2**20
         ),

time: 97.4 us -> 95.8 us (0.984)
  Pallas kernels: 94.4 us -> 92.6 us
    pallas_call x1, Pallas kernels: 94.4 us -> 92.6 us  [on_device(): pl.pallas_call(functools.partial(kernel, ny, nz, tr, tc), out_shape=[f32_...]
where the time goes in v4:
time: 95.8 us; the launch traced here: 95.1 us
  Pallas kernels  92.6 us (97%)
  other arithmetic  1.82 us (2%)
    pallas_call x1, Pallas kernels, on_device(): pl.pallas_call(functools.partial(kernel, ny, nz, tr, tc), out_shape=[f32_...  92.6 us

profile of v4, /device:TPU:24, one launch (start us, length us, event | category | flops | bytes accessed | tf_op | source)
XLA Modules:
  0.0 95.1 jit_solution(9667731613510195001)
XLA Ops:
  0.6 0.0 copy-start.1
  0.6 0.0 copy-start
  0.7 0.0 copy-start.2
  0.7 92.6 %shard_map.93 = (f32[256,128]{1,0:T(8,128)}, f32[256,128]{1,0:T(8,128)}) custom-call(bf16[256,128]{1,0:T(8,128)(2,1)} %g_hbm.1, bf16[128,256]{1,0:T(8,128)(2,1)} %l_hbm.1, bf16[256,128]{1,0:T(8,128)(2,1)} %r_hbm.1, f32[256,128]{1,0:T(8,128)} %m1_hbm.1, f32[256,128]{1,0:T(8,128)} %m2_hbm.1), custom_call_target="tpu_custom_call" | custom-call | tf_op jit(solution)/shard_map/pallas_call | solution.py:535
  93.3 0.0 copy-done.1
  93.3 0.0 copy-done
  93.3 0.0 copy-done.2
  93.3 1.8 %fusion = (f32[256,128]{1,0:T(8,128)}, f32[256,128]{1,0:T(8,128)}, f32[256,128]{1,0:T(8,128)}, bf16[256,128]{1,0:T(8,128)(2,1)}) fusion(f32[256,128]{1,0:T(8,128)} %get-tuple-element.7, f32[256,128]{1,0:T(8,128)S(1)} %copy-done.1, f32[256,128]{1,0:T(8,128)S(1)} %copy-done, f32[256,128]{1,0:T(8,128)S(1)} %copy-done.2, f32[256,128]{1,0:T(8,128)} %get-tuple-element.6), kind=kLoop, calls=%fused_computation.1 | loop fusion | flops 393216 | bytes 1114112 | tf_op jit(solution)/shard_map/add | solution.py:578
Async XLA Ops:
  0.6 92.6 %copy-start.1 = (f32[256,128]{1,0:T(8,128)S(1)}, f32[256,128]{1,0:T(8,128)}, u32[]{:S(2)}) copy-start(f32[256,128]{1,0:T(8,128)} %m2_hbm.1) | copy-start | bytes 393220
  0.6 92.6 %copy-start = (f32[256,128]{1,0:T(8,128)S(1)}, f32[256,128]{1,0:T(8,128)}, u32[]{:S(2)}) copy-start(f32[256,128]{1,0:T(8,128)} %m1_hbm.1) | copy-start | bytes 393220
  0.7 92.6 %copy-start.2 = (f32[256,128]{1,0:T(8,128)S(1)}, f32[256,128]{1,0:T(8,128)}, u32[]{:S(2)}) copy-start(f32[256,128]{1,0:T(8,128)} %param.11) | copy-start | bytes 393220

commit v5 on v4

--- a/solution.py
+++ b/solution.py
@@ -15,13 +15,13 @@
 step_count = 20.0
 
 MESH = pl.DeviceIdType.MESH
-G_UP, G_DN = (2, 2, 2, 1, 1), (2, 2, 2, 1)
+G_UP, G_DN = (2, 2, 2, 2), (2, 2, 2, 1)
 L_UP, L_DN = (1, 1, 1, 1, 1, 1, 1, 1), (1, 1, 1, 1, 1, 1, 1)
 U_UP, U_DN = (2, 2, 2, 2), (2, 2, 2, 1)
-LAG = 1
+LAG = 0
 PARTS = 2
 G_PARTS = 1
-RELAY_AT = 5
+RELAY_AT = 3
 L_PARTS = 2
 
 

time: 95.8 us -> 94.3 us (0.984)
  Pallas kernels: 92.6 us -> 91.6 us
    pallas_call x1, Pallas kernels: 92.6 us -> 91.6 us  [on_device(): pl.pallas_call(functools.partial(kernel, ny, nz, tr, tc), out_shape=[f32_...]
where the time goes in v5:
time: 94.3 us; the launch traced here: 94.1 us
  Pallas kernels  91.6 us (97%)
  other arithmetic  1.82 us (2%)
    pallas_call x1, Pallas kernels, on_device(): pl.pallas_call(functools.partial(kernel, ny, nz, tr, tc), out_shape=[f32_...  91.6 us

profile of v5, /device:TPU:24, one launch (start us, length us, event | category | flops | bytes accessed | tf_op | source)
XLA Modules:
  0.0 94.1 jit_solution(12079220291605146254)
XLA Ops:
  0.6 0.0 copy-start.1
  0.6 0.0 copy-start
  0.7 0.0 copy-start.2
  0.7 91.6 %shard_map.93 = (f32[256,128]{1,0:T(8,128)}, f32[256,128]{1,0:T(8,128)}) custom-call(bf16[256,128]{1,0:T(8,128)(2,1)} %g_hbm.1, bf16[128,256]{1,0:T(8,128)(2,1)} %l_hbm.1, bf16[256,128]{1,0:T(8,128)(2,1)} %r_hbm.1, f32[256,128]{1,0:T(8,128)} %m1_hbm.1, f32[256,128]{1,0:T(8,128)} %m2_hbm.1), custom_call_target="tpu_custom_call" | custom-call | tf_op jit(solution)/shard_map/pallas_call | solution.py:535
  92.2 0.0 copy-done.1
  92.2 0.0 copy-done
  92.3 0.0 copy-done.2
  92.3 1.8 %fusion = (f32[256,128]{1,0:T(8,128)}, f32[256,128]{1,0:T(8,128)}, f32[256,128]{1,0:T(8,128)}, bf16[256,128]{1,0:T(8,128)(2,1)}) fusion(f32[256,128]{1,0:T(8,128)} %get-tuple-element.7, f32[256,128]{1,0:T(8,128)S(1)} %copy-done.1, f32[256,128]{1,0:T(8,128)S(1)} %copy-done, f32[256,128]{1,0:T(8,128)S(1)} %copy-done.2, f32[256,128]{1,0:T(8,128)} %get-tuple-element.6), kind=kLoop, calls=%fused_computation.1 | loop fusion | flops 393216 | bytes 1114112 | tf_op jit(solution)/shard_map/add | solution.py:578
Async XLA Ops:
  0.6 91.6 %copy-start.1 = (f32[256,128]{1,0:T(8,128)S(1)}, f32[256,128]{1,0:T(8,128)}, u32[]{:S(2)}) copy-start(f32[256,128]{1,0:T(8,128)} %m2_hbm.1) | copy-start | bytes 393220
  0.6 91.6 %copy-start = (f32[256,128]{1,0:T(8,128)S(1)}, f32[256,128]{1,0:T(8,128)}, u32[]{:S(2)}) copy-start(f32[256,128]{1,0:T(8,128)} %m1_hbm.1) | copy-start | bytes 393220
  0.7 91.6 %copy-start.2 = (f32[256,128]{1,0:T(8,128)S(1)}, f32[256,128]{1,0:T(8,128)}, u32[]{:S(2)}) copy-start(f32[256,128]{1,0:T(8,128)} %param.11) | copy-start | bytes 393220
